TPU v7x, 32 devices: a whole 2x2x4 slice. The times are simulated.
32 devices in a mesh: img: 8 (over z, y), win: 4 (over x, core).
Axes of the slice: x: 2, y: 2, z: 4, core: 2. Of those that a mesh axis runs over, the one named last changes fastest.
Arguments:
- tokens: bfloat16 [256, 4, 49, 384], P('img', 'win'), may hold values from -6 to 6
- cotangent: bfloat16 [256, 4, 49, 384], P('img', 'win'), may hold values from -6 to 6
- crop_counts: int32 [8], P('img'), may hold values from 8 to 32, as said below
- crop_extent: int32 [256, 2], P('img'), may hold values from 10 to 14
- norm_gain: float32 [2, 2, 384], replicated, may hold values from 0.1 to 1.9
- norm_bias: float32 [2, 2, 384], replicated, may hold values from -3 to 3
- qkv_weight: bfloat16 [2, 384, 1152], replicated, may hold values from -0.3125 to 0.3125
- qv_bias: float32 [2, 2, 384], replicated, may hold values from -3 to 3
- rel_table: float32 [2, 169, 12], replicated, may hold values from -5 to 5
- proj_weight: bfloat16 [2, 384, 384], replicated, may hold values from -1.25 to 1.25
- out_bias: float32 [2, 2, 384], replicated, may hold values from -3 to 3
- fc1_weight: bfloat16 [2, 384, 1536], replicated, may hold values from -0.3125 to 0.3125
- fc1_bias: float32 [2, 1536], replicated, may hold values from -3 to 3
- fc2_weight: bfloat16 [2, 1536, 384], replicated, may hold values from -0.15625 to 0.15625
Outputs:
- output: bfloat16 [256, 4, 49, 384], P('img', 'win')
- input_grad: bfloat16 [256, 4, 49, 384], P('img', 'win')
- grad_norm_gain: float32 [2, 2, 384], replicated
- grad_norm_bias: float32 [2, 2, 384], replicated
- grad_qkv_weight: float32 [2, 384, 1152], replicated
- grad_qv_bias: float32 [2, 2, 384], replicated
- grad_rel_table: float32 [2, 169, 12], replicated
- grad_proj_weight: float32 [2, 384, 384], replicated
- grad_out_bias: float32 [2, 2, 384], replicated
- grad_fc1_weight: float32 [2, 384, 1536], replicated
- grad_fc1_bias: float32 [2, 1536], replicated
- grad_fc2_weight: float32 [2, 1536, 384], replicated
Inputs may be any that keep to these rules, and one draw needn't show every extreme that they name: `crop_counts`: slots of an image group from this count on are empty; in every draw some group is full.
All inputs are finite; a program needn't handle non-finite values.
Results may differ from a plain program's by a relative error of at most 0.017.
Values may be sent and summed in bfloat16 or wider, within the bound.
A program may use at most 256 MiB of HBM per device.

v0:
```python
from functools import partial

import jax
import jax.numpy as jnp
from jax import lax
from jax.sharding import PartitionSpec as P

D = 384
HEADS = 12
HEAD_DIM = 32
WINDOW = 7
SHIFT = 3


highest = lax.Precision.HIGHEST
norm_eps = 1e-05


def partner(value, axis, apart):
    mask = 2**apart
    pairs = [(source, source ^ mask) for source in range(lax.axis_size(axis))]
    return lax.ppermute(value, axis, pairs)


def norm_rows(values, gains, shifts):
    row_mean = jnp.mean(values, -1, keepdims=True)
    centred = values - row_mean
    row_var = jnp.mean(centred * centred, -1, keepdims=True)
    return centred * lax.rsqrt(row_var + norm_eps) * gains + shifts


def rows_grid(window_rows):
    return window_rows.reshape(window_rows.shape[0], WINDOW, WINDOW, window_rows.shape[-1])


def shift_in(window_rows):
    grid_here = rows_grid(window_rows)
    col_strip = partner(grid_here[:, :, :SHIFT], "win", 0)
    widened = jnp.concatenate([grid_here[:, :, SHIFT:], col_strip], 2)
    row_strip = partner(widened[:, :SHIFT], "win", 1)
    return jnp.concatenate([widened[:, SHIFT:], row_strip], 1).reshape(window_rows.shape)


def shift_out(window_rows):
    keep_cells = WINDOW - SHIFT
    grid_here = rows_grid(window_rows)
    col_strip = partner(grid_here[:, :, keep_cells:], "win", 0)
    widened = jnp.concatenate([col_strip, grid_here[:, :, :keep_cells]], 2)
    row_strip = partner(widened[:, keep_cells:], "win", 1)
    return jnp.concatenate([row_strip, widened[:, :keep_cells]], 1).reshape(window_rows.shape)


def position_lookup():
    places = jnp.arange(WINDOW * WINDOW)
    row_part = places // WINDOW
    col_part = places % WINDOW
    table_side = 2 * WINDOW - 1
    rel_index = (
        (row_part[:, None] - row_part[None, :] + WINDOW - 1) * table_side
        + col_part[:, None]
        - col_part[None, :]
        + WINDOW
        - 1
    ).reshape(-1)
    return (rel_index[:, None] == jnp.arange(table_side * table_side)[None, :]).astype(jnp.float32)


def block_parts(token_rows, crops_here, allowed, bias_heads, params):
    gains, shifts, w_qkv, qv_biases, w_proj, bias_pair, w_up, up_bias, w_down = params
    head_shape = (crops_here, WINDOW * WINDOW, HEADS, HEAD_DIM)
    normed = norm_rows(token_rows, gains[0], shifts[0]).astype(jnp.bfloat16)
    projected = jnp.dot(normed, w_qkv, preferred_element_type=jnp.float32)
    queries = (projected[:, :D] + qv_biases[0]).astype(jnp.bfloat16).reshape(head_shape)
    keys_low = projected[:, D : 2 * D].astype(jnp.bfloat16).reshape(head_shape)
    values = (projected[:, 2 * D :] + qv_biases[1]).astype(jnp.bfloat16).reshape(head_shape)
    scores = jnp.einsum("cihe,cjhe->chij", queries, keys_low, preferred_element_type=jnp.float32)
    scores = scores * HEAD_DIM ** (-0.5) + bias_heads
    scores = jnp.where(allowed[:, None], scores, -1e30)
    row_top = jnp.max(scores, -1, keepdims=True)
    exp_terms = jnp.exp(scores - row_top)
    attn_probs = exp_terms / jnp.sum(exp_terms, -1, keepdims=True)
    probs_low = attn_probs.astype(jnp.bfloat16)
    mixed_heads = jnp.einsum(
        "chij,cjhe->cihe", probs_low, values, preferred_element_type=jnp.float32
    )
    mixed_heads = mixed_heads.astype(jnp.bfloat16).reshape(-1, D)
    middle = token_rows + (
        jnp.dot(mixed_heads, w_proj, preferred_element_type=jnp.float32) + bias_pair[0]
    )
    normed_two = norm_rows(middle, gains[1], shifts[1]).astype(jnp.bfloat16)
    inner_pre = jnp.dot(normed_two, w_up, preferred_element_type=jnp.float32) + up_bias
    hidden = jax.nn.gelu(inner_pre, approximate=False).astype(jnp.bfloat16)
    result = middle + (jnp.dot(hidden, w_down, preferred_element_type=jnp.float32) + bias_pair[1])
    return (
        result,
        (
            normed,
            queries,
            keys_low,
            values,
            attn_probs,
            probs_low,
            mixed_heads,
            middle,
            normed_two,
            inner_pre,
            hidden,
        ),
    )


def block_backward(token_rows, crops_here, allowed, bias_heads, params, grad_rows):
    gains, shifts, w_qkv, qv_biases, w_proj, bias_pair, w_up, up_bias, w_down = params
    kept = block_parts(token_rows, crops_here, allowed, bias_heads, params)[1]
    (
        normed,
        queries,
        keys_low,
        values,
        attn_probs,
        probs_low,
        mixed_heads,
        middle,
        normed_two,
        inner_pre,
        hidden,
    ) = kept
    grad_low = grad_rows.astype(jnp.bfloat16)
    grad_down = jnp.einsum("rf,rd->fd", hidden, grad_low, preferred_element_type=jnp.float32)
    grad_down_bias = jnp.sum(grad_low, 0, dtype=jnp.float32)
    grad_hidden = jnp.einsum("rd,fd->rf", grad_low, w_down, preferred_element_type=jnp.float32)
    gelu_pull = jax.vjp(partial(jax.nn.gelu, approximate=False), inner_pre)[1]
    grad_inner = gelu_pull(grad_hidden)[0].astype(jnp.bfloat16)
    grad_up = jnp.einsum("rd,rf->df", normed_two, grad_inner, preferred_element_type=jnp.float32)
    grad_up_bias = jnp.sum(grad_inner, 0, dtype=jnp.float32)
    grad_normed_two = jnp.einsum("rf,df->rd", grad_inner, w_up, preferred_element_type=jnp.float32)
    norm_pull = jax.vjp(norm_rows, middle, gains[1], shifts[1])[1]
    grad_mid_norm, grad_gain_two, grad_shift_two = norm_pull(grad_normed_two)
    grad_middle = grad_rows + grad_mid_norm
    grad_branch = grad_middle.astype(jnp.bfloat16)
    grad_proj = jnp.einsum(
        "rd,re->de", mixed_heads, grad_branch, preferred_element_type=jnp.float32
    )
    grad_proj_bias = jnp.sum(grad_branch, 0, dtype=jnp.float32)
    grad_mixed = jnp.einsum("re,de->rd", grad_branch, w_proj, preferred_element_type=jnp.float32)
    grad_mixed = grad_mixed.astype(jnp.bfloat16).reshape(queries.shape)
    grad_probs = jnp.einsum(
        "cihe,cjhe->chij", grad_mixed, values, preferred_element_type=jnp.float32
    )
    grad_values = jnp.einsum(
        "chij,cihe->cjhe", probs_low, grad_mixed, preferred_element_type=jnp.float32
    ).astype(jnp.bfloat16)
    grad_scores = attn_probs * (grad_probs - jnp.sum(attn_probs * grad_probs, -1, keepdims=True))
    grad_scores = grad_scores.astype(jnp.bfloat16)
    grad_bias_heads = jnp.sum(grad_scores, 0, dtype=jnp.float32)
    attention_scale = HEAD_DIM ** (-0.5)
    grad_queries = (
        jnp.einsum("chij,cjhe->cihe", grad_scores, keys_low, preferred_element_type=jnp.float32)
        * attention_scale
    ).astype(jnp.bfloat16)
    grad_keys = (
        jnp.einsum("chij,cihe->cjhe", grad_scores, queries, preferred_element_type=jnp.float32)
        * attention_scale
    ).astype(jnp.bfloat16)
    grad_projected = jnp.concatenate(
        [grad_queries.reshape(-1, D), grad_keys.reshape(-1, D), grad_values.reshape(-1, D)], 1
    )
    grad_qkv = jnp.einsum("rd,re->de", normed, grad_projected, preferred_element_type=jnp.float32)
    grad_qv = jnp.stack(
        [
            jnp.sum(grad_projected[:, :D], 0, dtype=jnp.float32),
            jnp.sum(grad_projected[:, 2 * D :], 0, dtype=jnp.float32),
        ]
    )
    grad_normed = jnp.einsum("re,de->rd", grad_projected, w_qkv, preferred_element_type=jnp.float32)
    first_pull = jax.vjp(norm_rows, token_rows, gains[0], shifts[0])[1]
    grad_in_norm, grad_gain_one, grad_shift_one = first_pull(grad_normed)
    grad_input = grad_middle + grad_in_norm
    grad_terms = (
        jnp.stack([grad_gain_one, grad_gain_two]),
        jnp.stack([grad_shift_one, grad_shift_two]),
        grad_qkv,
        grad_qv,
        grad_bias_heads,
        grad_proj,
        jnp.stack([grad_proj_bias, grad_down_bias]),
        grad_up,
        grad_up_bias,
        grad_down,
    )
    return (grad_input, grad_terms)


def table_terms(grad_terms, lookup):
    grad_table = jnp.einsum(
        "pk,hp->kh", lookup, grad_terms[4].reshape(HEADS, -1), precision=highest
    )
    return grad_terms[:4] + (grad_table,) + grad_terms[5:]


def on_device(
    tokens,
    cotangent,
    crop_counts,
    crop_extent,
    norm_gain,
    norm_bias,
    qkv_weight,
    qv_bias,
    rel_table,
    proj_weight,
    out_bias,
    fc1_weight,
    fc1_bias,
    fc2_weight,
):
    crops_here = tokens.shape[0]
    window_cells = WINDOW * WINDOW
    grid_side = 2 * WINDOW
    window_index = lax.axis_index("win")
    places = jnp.arange(window_cells)
    row_here = WINDOW * (window_index // 2) + places // WINDOW
    col_here = WINDOW * (window_index % 2) + places % WINDOW
    extent_rows = crop_extent[:, 0:1]
    extent_cols = crop_extent[:, 1:2]
    plain_valid = ((row_here[None] < extent_rows) & (col_here[None] < extent_cols)).astype(
        jnp.int32
    )
    moved_valid = (
        (((row_here + SHIFT) % grid_side)[None] < extent_rows)
        & (((col_here + SHIFT) % grid_side)[None] < extent_cols)
    ).astype(jnp.int32)
    row_region = (row_here >= grid_side - WINDOW).astype(jnp.int32) + (
        row_here >= grid_side - SHIFT
    ).astype(jnp.int32)
    col_region = (col_here >= grid_side - WINDOW).astype(jnp.int32) + (
        col_here >= grid_side - SHIFT
    ).astype(jnp.int32)
    shifted_ids = 2 * (3 * row_region + col_region)[None] + moved_valid
    allowed_one = plain_valid[:, :, None] == plain_valid[:, None, :]
    allowed_two = shifted_ids[:, :, None] == shifted_ids[:, None, :]
    live_slot = (jnp.arange(crops_here) < crop_counts[0])[:, None, None]
    lookup = position_lookup()
    params_all = [
        (
            norm_gain[which],
            norm_bias[which],
            qkv_weight[which],
            qv_bias[which],
            proj_weight[which],
            out_bias[which],
            fc1_weight[which],
            fc1_bias[which],
            fc2_weight[which],
        )
        for which in (0, 1)
    ]
    bias_all = [
        jnp.einsum("pk,kh->hp", lookup, rel_table[which], precision=highest).reshape(
            HEADS, window_cells, window_cells
        )
        for which in (0, 1)
    ]
    token_rows = tokens.reshape(-1, D).astype(jnp.float32)
    first_out = block_parts(token_rows, crops_here, allowed_one, bias_all[0], params_all[0])[0]
    rolled_low = shift_in(first_out.astype(jnp.bfloat16).reshape(crops_here, window_cells, D))
    rolled_rows = rolled_low.reshape(-1, D).astype(jnp.float32)
    second_out = block_parts(rolled_rows, crops_here, allowed_two, bias_all[1], params_all[1])[0]
    output = shift_out(second_out.astype(jnp.bfloat16).reshape(crops_here, window_cells, D))
    output = jnp.where(live_slot, output, jnp.zeros_like(output)).reshape(tokens.shape)
    cot_rows = cotangent.reshape(crops_here, window_cells, D)
    cot_rows = jnp.where(live_slot, cot_rows, jnp.zeros_like(cot_rows))
    grad_rolled = shift_in(cot_rows).reshape(-1, D).astype(jnp.float32)
    grad_second, terms_two = block_backward(
        rolled_rows, crops_here, allowed_two, bias_all[1], params_all[1], grad_rolled
    )
    terms_two = table_terms(terms_two, lookup)
    grad_first = shift_out(grad_second.astype(jnp.bfloat16).reshape(crops_here, window_cells, D))
    grad_first = grad_first.reshape(-1, D).astype(jnp.float32)
    grad_input, terms_one = block_backward(
        token_rows, crops_here, allowed_one, bias_all[0], params_all[0], grad_first
    )
    terms_one = table_terms(terms_one, lookup)
    stacked = tuple(
        (jnp.stack([left_term, right_term]) for left_term, right_term in zip(terms_one, terms_two))
    )
    summed = lax.psum(
        (
            stacked[0],
            stacked[1],
            stacked[2],
            stacked[3],
            stacked[4],
            stacked[5],
            stacked[6],
            stacked[7],
            stacked[8],
            stacked[9],
        ),
        ("img", "win"),
    )
    input_grad = grad_input.astype(jnp.bfloat16).reshape(tokens.shape)
    return (
        output,
        input_grad,
        summed[0],
        summed[1],
        summed[2],
        summed[3],
        summed[4],
        summed[5],
        summed[6],
        summed[7],
        summed[8],
        summed[9],
    )


def solution(mesh):
    placed = (
        P("img", "win", None, None),
        P("img", "win", None, None),
        P("img"),
        P("img", None),
        P(),
        P(),
        P(),
        P(),
        P(),
        P(),
        P(),
        P(),
        P(),
        P(),
    )
    return jax.shard_map(
        on_device,
        mesh=mesh,
        in_specs=placed,
        out_specs=(
            P("img", "win", None, None),
            P("img", "win", None, None),
            P(),
            P(),
            P(),
            P(),
            P(),
            P(),
            P(),
            P(),
            P(),
            P(),
        ),
        check_vma=False,
    )
```

profile of v0, /device:TPU:0, one launch (start us, length us, event | category | flops | bytes accessed | tf_op | source)
XLA Modules:
  0.0 883.0 jit_solution(7153395389890641172)
XLA Ops:
  39.9 10.2 %reshape.824 = bf16[32,49,12,32]{1,0,3,2:T(8,128)(2,1)} reshape(bf16[1568,384]{0,1:T(8,128)(2,1)S(1)} %copy.227) | data formatting | bytes 2408448 | tf_op jit(solution)/shard_map/reshape | solution.py:75
  50.1 10.3 %reshape.826 = bf16[32,49,12,32]{1,0,3,2:T(8,128)(2,1)S(1)} reshape(bf16[1568,384]{0,1:T(8,128)(2,1)} %copy.229) | data formatting | bytes 2408448 | tf_op jit(solution)/shard_map/reshape | solution.py:74
  60.4 11.6 %reshape.825 = bf16[32,49,12,32]{1,0,3,2:T(8,128)(2,1)} reshape(bf16[1568,384]{0,1:T(8,128)(2,1)} %copy.228) | data formatting | bytes 2408448 | tf_op jit(solution)/shard_map/reshape | solution.py:73
  72.0 13.5 %fusion.57 = f32[32,12,49,49]{2,3,1,0:T(8,128)} fusion(bf16[32,49,12,32]{1,0,3,2:T(8,128)(2,1)S(1)} %reshape.826, bf16[32,49,12,32]{1,0,3,2:T(8,128)(2,1)} %reshape.825), kind=kOutput, calls=%fused_computation.128 | convolution fusion | flops 59006976 | bytes 6096384 | tf_op jit(solution)/shard_map/cihe,cjhe->chij/dot_general | solution.py:76
  85.5 13.1 %fusion.178 = (f32[32,12,49]{2,1,0:T(8,128)S(1)}, f32[32,12,49,49]{2,3,1,0:T(8,128)S(1)}) fusion(f32[32,12,49,49]{2,3,1,0:T(8,128)} %fusion.57, f32[12,49,49]{1,2,0:T(8,128)S(1)} %copy-done.58, pred[32,49,49]{1,2,0:T(8,128)(4,1)S(1)} %broadcast_compare_fusion.1), kind=kOutput, calls=%fused_computation.349 | output fusion | flops 7375920 | bytes 7643216 | tf_op jit(solution)/shard_map/sub | solution.py:80
  120.6 25.1 %multiply_convert_fusion.3 = (bf16[1568,1536]{1,0:T(8,128)(2,1)S(1)}, f32[1568,1536]{1,0:T(8,128)}, f32[1568,1536]{1,0:T(8,128)}) fusion(f32[1536]{0:T(1024)S(1)} %get-tuple-element.85, bf16[2,384,1536]{2,1,0:T(8,128)(2,1)S(1)} %copy-done.125, f32[1568,384]{1,0:T(8,128)S(1)} %get-tuple-element.149, f32[384]{0:T(512)S(1)} %get-tuple-element.95, ...), kind=kOutput, calls=%fused_computation.33 | convolution fusion | flops 2011656192 | bytes 27701248 | tf_op jit(solution)/shard_map/dot_general | solution.py:91
  205.1 10.6 %reshape.828 = bf16[32,49,12,32]{1,0,3,2:T(8,128)(2,1)} reshape(bf16[1568,384]{0,1:T(8,128)(2,1)S(1)} %copy.241) | data formatting | bytes 2408448 | tf_op jit(solution)/shard_map/reshape | solution.py:75
  215.7 10.3 %reshape.830 = bf16[32,49,12,32]{1,0,3,2:T(8,128)(2,1)S(1)} reshape(bf16[1568,384]{0,1:T(8,128)(2,1)} %copy.243) | data formatting | bytes 2408448 | tf_op jit(solution)/shard_map/reshape | solution.py:74
  225.9 11.4 %reshape.829 = bf16[32,49,12,32]{1,0,3,2:T(8,128)(2,1)} reshape(bf16[1568,384]{0,1:T(8,128)(2,1)} %copy.242) | data formatting | bytes 2408448 | tf_op jit(solution)/shard_map/reshape | solution.py:73
  237.3 13.3 %fusion.47 = f32[32,12,49,49]{2,3,1,0:T(8,128)} fusion(bf16[32,49,12,32]{1,0,3,2:T(8,128)(2,1)S(1)} %reshape.830, bf16[32,49,12,32]{1,0,3,2:T(8,128)(2,1)} %reshape.829), kind=kOutput, calls=%fused_computation.118 | convolution fusion | flops 59006976 | bytes 6096384 | tf_op jit(solution)/shard_map/cihe,cjhe->chij/dot_general | solution.py:76
  250.7 12.9 %fusion.180 = (f32[32,12,49]{2,1,0:T(8,128)S(1)}, f32[32,12,49,49]{2,3,1,0:T(8,128)S(1)}) fusion(f32[32,12,49,49]{2,3,1,0:T(8,128)} %fusion.47, f32[12,49,49]{1,2,0:T(8,128)S(1)} %copy-done.57, pred[32,49,49]{1,2,0:T(8,128)(4,1)S(1)} %copy-done.62), kind=kOutput, calls=%fused_computation.351 | output fusion | flops 7375920 | bytes 7643216 | tf_op jit(solution)/shard_map/sub | solution.py:80
  285.7 24.8 %multiply_convert_fusion.2 = (bf16[1568,1536]{1,0:T(8,128)(2,1)}, f32[1568,1536]{1,0:T(8,128)S(1)}, f32[1568,1536]{1,0:T(8,128)}) fusion(f32[1536]{0:T(1024)S(1)} %copy-done.94, bf16[2,384,1536]{2,1,0:T(8,128)(2,1)S(1)} %copy-done.126, f32[1568,384]{1,0:T(8,128)S(1)} %get-tuple-element.154, f32[384]{0:T(512)S(1)} %copy-done.115, f32[384]{0:T(512)S(1)} %copy-done.104, ...), kind=kOutput, calls=%fused_computation.20 | convolution fusion | flops 2011656192 | bytes 27701248 | tf_op jit(solution)/shard_map/dot_general | solution.py:91
  310.5 8.8 convert_reduce_fusion.2
  335.5 11.3 %reshape.834 = bf16[32,49,12,32]{1,0,3,2:T(8,128)(2,1)} reshape(bf16[1568,384]{0,1:T(8,128)(2,1)} %copy.257) | data formatting | bytes 2408448 | tf_op jit(solution)/shard_map/reshape | solution.py:146
  346.8 11.3 %convert_reduce_fusion.4 = (f32[12,32]{1,0:T(8,128)}, bf16[32,49,12,32]{1,3,2,0:T(8,128)(2,1)}) fusion(f32[32,12,49,49]{2,3,1,0:T(8,128)} %copy-done.16, f32[32,12,49]{2,1,0:T(8,128)S(1)} %get-tuple-element.151, bf16[32,49,12,32]{1,0,3,2:T(8,128)(2,1)} %reshape.834), kind=kOutput, calls=%fused_computation.52 | convolution fusion | flops 62656896 | bytes 6173184 | tf_op jit(solution)/shard_map/chij,cihe->cjhe/dot_general | solution.py:150
  358.2 15.8 %multiply_reduce_fusion.1 = (f32[32,12,49]{2,1,0:T(8,128)S(1)}, f32[32,12,49,49]{2,3,1,0:T(8,128)}) fusion(f32[32,12,49,49]{2,3,1,0:T(8,128)} %copy-done.16, f32[32,12,49]{2,1,0:T(8,128)S(1)} %get-tuple-element.151, bf16[32,49,12,32]{1,0,3,2:T(8,128)(2,1)S(1)} %copy-done.38, bf16[32,49,12,32]{1,0,3,2:T(8,128)(2,1)} %reshape.834), kind=kOutput, calls=%fused_computation.9 | convolution fusion | flops 61754112 | bytes 9934848 | tf_op jit(solution)/shard_map/cihe,cjhe->chij/dot_general | solution.py:147
  374.0 9.5 %convert_reduce_fusion = (f32[12,49,49]{1,2,0:T(8,128)S(1)}, bf16[32,12,49,49]{2,3,1,0:T(8,128)(2,1)S(1)}) fusion(f32[32,12,49,49]{2,3,1,0:T(8,128)} %get-tuple-element.158, f32[32,12,49]{2,1,0:T(8,128)S(1)} %get-tuple-element.157, f32[32,12,49,49]{2,3,1,0:T(8,128)} %copy-done.16, f32[32,12,49]{2,1,0:T(8,128)} %copy-done.61), kind=kLoop, calls=%fused_computation.4 | loop fusion | flops 5503092 | bytes 9485616 | tf_op jit(solution)/shard_map/reduce_sum | solution.py:155
  476.3 10.1 %convert_reduce_fusion.3 = (f32[1536]{0:T(1024)}, bf16[1568,1536]{1,0:T(8,128)(2,1)S(1)}) fusion(f32[1568,1536]{1,0:T(8,128)} %get-tuple-element.133, f32[1568,1536]{1,0:T(8,128)} %get-tuple-element.150, bf16[1568,384]{1,0:T(8,128)(2,1)S(1)} %reshape_reshape.20, bf16[2,1536,384]{2,1,0:T(8,128)(2,1)S(1)} %copy-done.130), kind=kOutput, calls=%fused_computation.17 | convolution fusion | flops 1888221696 | bytes 26474496 | tf_op jit(solution)/shard_map/rd,fd->rf/dot_general | solution.py:131
  502.9 11.5 %reshape.838 = bf16[32,49,12,32]{1,0,3,2:T(8,128)(2,1)} reshape(bf16[1568,384]{0,1:T(8,128)(2,1)} %copy.273) | data formatting | bytes 2408448 | tf_op jit(solution)/shard_map/reshape | solution.py:146
  514.4 11.4 %convert_reduce_fusion.6 = (f32[12,32]{1,0:T(8,128)}, bf16[32,49,12,32]{1,3,2,0:T(8,128)(2,1)}) fusion(f32[32,12,49,49]{2,3,1,0:T(8,128)} %copy-done.15, f32[32,12,49]{2,1,0:T(8,128)S(1)} %copy-done.60, bf16[32,49,12,32]{1,0,3,2:T(8,128)(2,1)} %reshape.838), kind=kOutput, calls=%fused_computation.54 | convolution fusion | flops 62656896 | bytes 6173184 | tf_op jit(solution)/shard_map/chij,cihe->cjhe/dot_general | solution.py:150
  525.8 15.8 %multiply_reduce_fusion = (f32[32,12,49]{2,1,0:T(8,128)S(1)}, f32[32,12,49,49]{2,3,1,0:T(8,128)}) fusion(f32[32,12,49,49]{2,3,1,0:T(8,128)} %copy-done.15, f32[32,12,49]{2,1,0:T(8,128)S(1)} %copy-done.60, bf16[32,49,12,32]{1,0,3,2:T(8,128)(2,1)S(1)} %copy-done.37, bf16[32,49,12,32]{1,0,3,2:T(8,128)(2,1)} %reshape.838), kind=kOutput, calls=%fused_computation.7 | convolution fusion | flops 61754112 | bytes 9934848 | tf_op jit(solution)/shard_map/cihe,cjhe->chij/dot_general | solution.py:147
  541.5 10.0 %convert_reduce_fusion.1 = (f32[12,49,49]{1,2,0:T(8,128)}, bf16[32,12,49,49]{2,3,1,0:T(8,128)(2,1)S(1)}) fusion(f32[32,12,49,49]{2,3,1,0:T(8,128)} %get-tuple-element.162, f32[32,12,49]{2,1,0:T(8,128)S(1)} %get-tuple-element.161, f32[32,12,49,49]{2,3,1,0:T(8,128)} %copy-done.15, f32[32,12,49]{2,1,0:T(8,128)S(1)} %copy-done.60), kind=kLoop, calls=%fused_computation.5 | loop fusion | flops 5503092 | bytes 9485616 | tf_op jit(solution)/shard_map/reduce_sum | solution.py:155
  663.7 44.1 %all-reduce = (f32[2,2,384]{2,1,0:T(2,128)}, f32[2,2,384]{2,1,0:T(2,128)}, f32[2,2,384]{2,1,0:T(2,128)}, f32[2,169,12]{1,2,0:T(8,128)S(1)}, f32[2,2,384]{2,1,0:T(2,128)}, /*index=5*/f32[2,1536]{1,0:T(2,128)}) all-reduce(f32[2,2,384]{2,1,0:T(2,128)S(1)} %pad_maximum_fusion.14, ...), channel_id=1, replica_groups=mesh['img'=8,'win'=4] {'img','win'}, use_global_device_ids=true, to_apply=%region_26.27 | all-reduce | flops 13272 | bytes 106176 | tf_op jit(solution)/shard_map/psum | solution.py:287
  717.6 147.2 %all-reduce.4.cloned.1.call-done = (f32[2,384,1152]{2,1,0:T(8,128)}, f32[2,384,384]{2,1,0:T(8,128)}, f32[2,384,1536]{2,1,0:T(8,128)}, f32[2,1536,384]{2,1,0:T(8,128)}) async-done(((f32[2,384,1152]{2,1,0:T(8,128)}, f32[2,384,384]{2,1,0:T(8,128)}, f32[2,384,1536]{2,1,0:T(8,128)}, f32[2,1536,384]{2,1,0:T(8,128)}), (f32[2,384,1152]{2,1,0:T(8,128)}, f32[2,384,384]{2,1,0:T(8,128)}, f32[2,384,1536]{2,1,0:T(8,128)}, ...) | async-done | bytes 14155792 | tf_op jit(solution)/shard_map/psum | solution.py:287
  (510 shorter events, 392.2 us)
Async XLA Ops:
  7.2 857.6 %all-reduce.4.cloned.1.call-start = ((), (), s32[]{:S(2)}) async-start(), calls=%async_computation | async-start | bytes 28311552 | tf_op jit(solution)/shard_map/psum | solution.py:287
  11.4 154.2 %collective-permute-start.4 = (bf16[32,7,3,384]{3,0,2,1:T(8,128)(2,1)}, bf16[32,7,3,384]{3,0,2,1:T(8,128)(2,1)}, u32[]{:S(2)}, u32[]{:S(2)}) collective-permute-start(bf16[32,7,3,384]{3,0,2,1:T(8,128)(2,1)} %slice.293), channel_id=1, source_target_pairs={{0,1},{1,0},{2,3},{3,2},{4,5},{5,4},{6,7},{7,6},{8,9},{9,8},{10,11... | collective-permute-start | bytes 1548296 | tf_op jit(solution)/shard_map/ppermute | solution.py:22
  21.6 99.0 %copy-start.102 = (f32[384]{0:T(512)}, f32[384]{0:T(512)S(1)}, u32[]{:S(2)}) copy-start(f32[384]{0:T(512)S(1)} %get-tuple-element.178) | copy-start | bytes 4612
  21.6 99.0 %copy-start.113 = (f32[384]{0:T(512)}, f32[384]{0:T(512)S(1)}, u32[]{:S(2)}) copy-start(f32[384]{0:T(512)S(1)} %get-tuple-element.95) | copy-start | bytes 4612
  60.4 25.1 %copy-start = (bf16[32,49,12,32]{1,0,3,2:T(8,128)(2,1)}, bf16[32,49,12,32]{1,0,3,2:T(8,128)(2,1)S(1)}, u32[]{:S(2)}) copy-start(bf16[32,49,12,32]{1,0,3,2:T(8,128)(2,1)S(1)} %reshape.826) | copy-start | bytes 3612676
  119.9 25.8 %copy-start.11 = (f32[1568,384]{1,0:T(8,128)}, f32[1568,384]{1,0:T(8,128)S(1)}, u32[]{:S(2)}) copy-start(f32[1568,384]{1,0:T(8,128)S(1)} %get-tuple-element.149) | copy-start | bytes 7225348
  119.9 25.7 %copy-start.67 = (f32[1568]{0:T(1024)}, f32[1568]{0:T(1024)S(1)}, u32[]{:S(2)}) copy-start(f32[1568]{0:T(1024)S(1)} %broadcast_multiply_fusion.3) | copy-start | bytes 18820
  120.5 25.2 %copy-start.63 = (f32[1568]{0:T(1024)}, f32[1568]{0:T(1024)S(1)}, u32[]{:S(2)}) copy-start(f32[1568]{0:T(1024)S(1)} %multiply_reduce_fusion.12) | copy-start | bytes 18820
  120.5 25.2 %copy-start.72 = (f32[1568]{0:T(1024)}, f32[1568]{0:T(1024)S(1)}, u32[]{:S(2)}) copy-start(f32[1568]{0:T(1024)S(1)} %fusion.154) | copy-start | bytes 18820
  120.6 27.3 %copy-start.128 = (bf16[2,1536,384]{2,1,0:T(8,128)(2,1)S(1)}, bf16[2,1536,384]{2,1,0:T(8,128)(2,1)}, u32[]{:S(2)}) copy-start(bf16[2,1536,384]{2,1,0:T(8,128)(2,1)} %param.27) | copy-start | bytes 7077892
  155.2 4.6 collective-permute-start
  161.6 15.6 %collective-permute-start.1 = (bf16[32,3,7,384]{3,0,2,1:T(8,128)(2,1)S(1)}, bf16[32,3,7,384]{3,0,2,1:T(8,128)(2,1)S(1)}, u32[]{:S(2)}, u32[]{:S(2)}) collective-permute-start(bf16[32,3,7,384]{3,0,2,1:T(8,128)(2,1)S(1)} %copy.239), channel_id=1, source_target_pairs={{0,2},{1,3},{2,0},{3,1},{4,6},{5,7},{6,4},{7,5},{8,10},{9,11},{10,... | collective-permute-start | bytes 1548296 | tf_op jit(solution)/shard_map/ppermute | solution.py:22
  167.4 20.2 %collective-permute-start.5 = (bf16[32,3,7,384]{3,0,2,1:T(8,128)(2,1)}, bf16[32,3,7,384]{3,0,2,1:T(8,128)(2,1)S(1)}, u32[]{:S(2)}, u32[]{:S(2)}) collective-permute-start(bf16[32,3,7,384]{3,0,2,1:T(8,128)(2,1)} %pad_maximum_fusion.11), channel_id=1, source_target_pairs={{0,2},{1,3},{2,0},{3,1},{4,6},{5,7},{6,4},{7,5},{8,10},{9,11},{10,... | collective-permute-start | bytes 1548296 | tf_op jit(solution)/shard_map/ppermute | solution.py:22
  168.4 19.1 %copy-start.25 = (bf16[32,4,7,384]{3,0,2,1:T(8,128)(2,1)}, bf16[32,4,7,384]{3,0,2,1:T(8,128)(2,1)S(1)}, u32[]{:S(2)}) copy-start(bf16[32,4,7,384]{3,0,2,1:T(8,128)(2,1)S(1)} %fusion.145) | copy-start | bytes 2064388
  225.9 24.8 %copy-start.3 = (bf16[32,49,12,32]{1,0,3,2:T(8,128)(2,1)}, bf16[32,49,12,32]{1,0,3,2:T(8,128)(2,1)S(1)}, u32[]{:S(2)}) copy-start(bf16[32,49,12,32]{1,0,3,2:T(8,128)(2,1)S(1)} %reshape.830) | copy-start | bytes 3612676
  263.6 94.6 %copy-start.61 = (f32[32,12,49]{2,1,0:T(8,128)}, f32[32,12,49]{2,1,0:T(8,128)S(1)}, u32[]{:S(2)}) copy-start(f32[32,12,49]{2,1,0:T(8,128)S(1)} %get-tuple-element.151) | copy-start | bytes 225796
  285.0 42.1 %copy-start.13 = (f32[1568,384]{1,0:T(8,128)}, f32[1568,384]{1,0:T(8,128)S(1)}, u32[]{:S(2)}) copy-start(f32[1568,384]{1,0:T(8,128)S(1)} %get-tuple-element.154) | copy-start | bytes 7225348
  285.6 24.8 %copy-start.21 = (bf16[1568,384]{1,0:T(8,128)(2,1)S(1)}, bf16[1568,384]{1,0:T(8,128)(2,1)}, u32[]{:S(2)}) copy-start(bf16[1568,384]{1,0:T(8,128)(2,1)} %reshape_reshape.18) | copy-start | bytes 3612676
  285.7 24.8 %copy-start.129 = (bf16[2,1536,384]{2,1,0:T(8,128)(2,1)S(1)}, bf16[2,1536,384]{2,1,0:T(8,128)(2,1)}, u32[]{:S(2)}) copy-start(bf16[2,1536,384]{2,1,0:T(8,128)(2,1)} %param.27) | copy-start | bytes 7077892
  445.1 7.0 collective-permute-start.6
  452.9 14.2 %collective-permute-start.7 = (bf16[32,3,7,384]{3,0,2,1:T(8,128)(2,1)S(1)}, bf16[32,3,7,384]{3,0,2,1:T(8,128)(2,1)S(1)}, u32[]{:S(2)}, u32[]{:S(2)}) collective-permute-start(bf16[32,3,7,384]{3,0,2,1:T(8,128)(2,1)S(1)} %copy.271), channel_id=1, source_target_pairs={{0,2},{1,3},{2,0},{3,1},{4,6},{5,7},{6,4},{7,5},{8,10},{9,11},{10,... | collective-permute-start | bytes 1548296 | tf_op jit(solution)/shard_map/ppermute | solution.py:22
  626.2 2.0 collective-permute-start.2
  630.5 19.2 %collective-permute-start.3 = (bf16[32,3,7,384]{3,0,2,1:T(8,128)(2,1)}, bf16[32,3,7,384]{3,0,2,1:T(8,128)(2,1)}, u32[]{:S(2)}, u32[]{:S(2)}) collective-permute-start(bf16[32,3,7,384]{3,0,2,1:T(8,128)(2,1)} %copy.253), channel_id=1, source_target_pairs={{0,2},{1,3},{2,0},{3,1},{4,6},{5,7},{6,4},{7,5},{8,10},{9,11},{10,... | collective-permute-start | bytes 1548296 | tf_op jit(solution)/shard_map/ppermute | solution.py:22
  654.5 53.9 %copy-start.66 = (f32[1568]{0:T(1024)S(1)}, f32[1568]{0:T(1024)}, u32[]{:S(2)}) copy-start(f32[1568]{0:T(1024)} %copy-done.65) | copy-start | bytes 18820
  (121 other events, 586.7 us)
Sparse Core Ops, SparseCore 0:
  613.2 251.5 all-reduce.3
where the time goes:
time: 889 us; the launch traced here: 883 us
  local copies, waits for them, and re-layouts  275 us (31%)
  matrix products  270 us (30%)
  waiting for transfers between devices  178 us (20%)
  other arithmetic  91.9 us (10%)
  blocking collectives  44.1 us (5%)
  between operations  17.1 us (2%)
    psum x1, waiting for transfers between devices, on_device(): lax.psum((stacked[0], stacked[1], stacked[2], stacked[3], stacked[4], sta...  147 us
    dot_general x2, matrix products, block_parts(): jnp.dot(normed_two, w_up, preferred_element_type=jnp.float32) + up_bias  49.9 us
    psum x1, blocking collectives, on_device(): lax.psum((stacked[0], stacked[1], stacked[2], stacked[3], stacked[4], sta...  44.1 us
    dot_general x2, matrix products, block_backward(): jnp.einsum('cihe,cjhe->chij', grad_mixed, values, preferred_element_type=...  31.6 us
    ppermute x8, waiting for transfers between devices, partner(): return lax.ppermute(value, axis, pairs)  30.5 us
    dot_general x2, matrix products, block_parts(): jnp.einsum('cihe,cjhe->chij', queries, keys_low, preferred_element_type=j...  26.8 us
    unnamed x282, local copies, waits for them, and re-layouts  26.5 us
    sub x2, other arithmetic, block_parts(): exp_terms = jnp.exp(scores - row_top)  25.9 us
  transfers between devices with their start and end apart: 9, of which 5 were waited for; matrix products, arithmetic and copies ran while one was open for 24% of the time, Pallas kernels for 0%

commit v1 on v0

v1 whole, which is shorter than its diff:
```python
import jax
import jax.numpy as jnp
from jax import lax
from jax.experimental import pallas as pl
from jax.experimental.pallas import tpu as pltpu
from jax.sharding import PartitionSpec as P

D = 384
FF = 1536
HEADS = 12
HEAD_DIM = 32
WINDOW = 7
SHIFT = 3
CELLS = WINDOW * WINDOW
SIDE = 2 * WINDOW
HALF = 16
ROWS = CELLS * HALF
LANES = 128
GROUPS = 3
KEYS = 56
SLOT = 64
SLABS = 12
NEG = -1e30
LOG2E = 1.4426950408889634
SCALE = HEAD_DIM**-0.5
MESH = pl.DeviceIdType.MESH

bf16 = jnp.bfloat16
f32 = jnp.float32
VMEM = pltpu.VMEM


def mm(a, b):
    return lax.dot_general(a, b, (((1,), (0,)), ((), ())), preferred_element_type=f32)


def mm_bt(a, b):
    return lax.dot_general(a, b, (((1,), (1,)), ((), ())), preferred_element_type=f32)


def mm_at(a, b):
    return lax.dot_general(a, b, (((0,), (0,)), ((), ())), preferred_element_type=f32)


def norm(x):
    centred = x - jnp.mean(x, -1, keepdims=True)
    rstd = lax.rsqrt(jnp.mean(centred * centred, -1, keepdims=True) + 1e-5)
    return centred * rstd, rstd


def norm_back(xh, rstd, dn, gain):
    e = dn * gain
    mean_e = jnp.mean(e, -1, keepdims=True)
    mean_ex = jnp.mean(e * xh, -1, keepdims=True)
    dx = rstd * (e - mean_e - xh * mean_ex)
    return dx, jnp.sum(dn * xh, 0, keepdims=True), jnp.sum(dn, 0, keepdims=True)


def gelu(u):
    phi = 0.5 + 0.5 * lax.erf(u * 0.7071067811865476)
    return u * phi, phi


def gelu_slope(u, phi):
    return phi + u * jnp.exp2(u * u * (-0.5 * LOG2E)) * 0.3989422804014327


def spread(rows):
    head = lax.broadcasted_iota(jnp.int32, rows.shape, 1) // HEAD_DIM
    zero = jnp.zeros_like(rows)
    return jnp.concatenate([jnp.where(head == h, rows, zero) for h in range(4)], 0)


def gather_heads(rows):
    head = lax.broadcasted_iota(jnp.int32, (KEYS, LANES), 1) // HEAD_DIM
    out = rows[:KEYS]
    for h in range(1, 4):
        out = jnp.where(head == h, rows[SLOT * h : SLOT * h + KEYS], out)
    return out


def to_windows(ref, slot, part):
    parted = part.reshape(CELLS, 2, 8, LANES)
    for cg in range(2):
        ref[cg, slot, 0 : CELLS * 8, :] = parted[:, cg].reshape(CELLS * 8, LANES)


def from_windows(ref, slot):
    parts = [ref[cg, slot, 0 : CELLS * 8, :].reshape(CELLS, 1, 8, LANES) for cg in range(2)]
    return jnp.concatenate(parts, 1).reshape(ROWS, LANES)


def cells(shifted):
    win = lax.axis_index("win")
    j = lax.broadcasted_iota(jnp.int32, (KEYS, LANES), 0)
    i = lax.broadcasted_iota(jnp.int32, (KEYS, LANES), 1) % SLOT
    top, left = WINDOW * (win // 2), WINDOW * (win % 2)
    places = [top + j // WINDOW, left + j % WINDOW, top + i // WINDOW, left + i % WINDOW]
    if not shifted:
        return places, None
    region = [(v >= SIDE - WINDOW).astype(jnp.int32) + (v >= SIDE - SHIFT).astype(jnp.int32) for v in places]
    apart = (region[0] != region[2]) | (region[1] != region[3])
    moved = [jnp.where(v + SHIFT >= SIDE, v + SHIFT - SIDE, v + SHIFT) for v in places]
    return moved, jnp.where(apart, NEG, 0.0)


def forward(step, block, shifted, x, refs, keep_n1=None, keep_n2=None, keep_gelu=None, keep_u=None):
    (ext, gain, beta, wqkv, qvb, bias, wp, ob, w1, b1, w2, xs, qw, ss, pr, os, o16, mid) = refs
    xh, _ = norm(x)
    n1 = (xh * gain[block, 0:1, :] + beta[block, 0:1, :]).astype(bf16)
    if keep_n1 is not None:
        keep_n1[step] = n1
    proj = mm(n1, wqkv[...])
    q = (proj[:, :D] + qvb[block, 0:1, :]) * (SCALE * LOG2E)
    k = proj[:, D : 2 * D]
    v = proj[:, 2 * D :] + qvb[block, 1:2, :]
    for g in range(GROUPS):
        cut = slice(LANES * g, LANES * (g + 1))
        to_windows(xs, g, q[:, cut])
        to_windows(xs, GROUPS + g, k[:, cut])
        to_windows(xs, 2 * GROUPS + g, v[:, cut])
    places, apart = cells(shifted)
    if apart is not None:
        apart = jnp.concatenate([apart, apart], 1)

    def scores(w, carry):
        cg, c = w // 8, w % 8
        rows, cols = ext[step * HALF + w, 0], ext[step * HALF + w, 1]
        valid_j = (places[0] < rows) & (places[1] < cols)
        valid_i = (places[2] < rows) & (places[3] < cols)
        mask = jnp.where(valid_i == valid_j, 0.0, NEG)
        mask = jnp.concatenate([mask, mask], 1)
        if apart is not None:
            mask = mask + apart
        for g in range(GROUPS):
            qs, ks, vs = (
                xs[cg, GROUPS * n + g, pl.ds(c, SLOT, stride=8), :].astype(bf16) for n in range(3)
            )
            qw[w, g] = qs
            qw[w, GROUPS + g] = ks
            qw[w, 2 * GROUPS + g] = vs
            ss[w, g] = mm_bt(ks[:KEYS], spread(qs)) + bias[g] + mask
        return carry

    lax.fori_loop(0, HALF, scores, 0, unroll=2)

    def softmax(w, carry):
        for g in range(GROUPS):
            s = ss[w, g]
            e = jnp.exp2(s - jnp.max(s, 0, keepdims=True))
            pr[w, g] = (e * (1.0 / jnp.sum(e, 0, keepdims=True))).astype(bf16)
        return carry

    lax.fori_loop(0, HALF, softmax, 0)

    def mix(w, carry):
        cg, c = w // 8, w % 8
        for g in range(GROUPS):
            os[cg, g, pl.ds(c, KEYS, stride=8), :] = gather_heads(
                mm_at(pr[w, g], qw[w, 2 * GROUPS + g][:KEYS])
            )
        return carry

    lax.fori_loop(0, HALF, mix, 0)
    for g in range(GROUPS):
        o16[:, LANES * g : LANES * (g + 1)] = from_windows(os, g).astype(bf16)
    middle = x + (mm(o16[...], wp[...]) + ob[block, 0:1, :])
    mid[...] = middle
    xh2, _ = norm(middle)
    n2 = (xh2 * gain[block, 1:2, :] + beta[block, 1:2, :]).astype(bf16)
    if keep_n2 is not None:
        keep_n2[step] = n2
    y = middle + ob[block, 1:2, :]
    for part in range(3):
        cut = slice(512 * part, 512 * (part + 1))
        u = mm(n2, w1[:, cut]) + b1[block : block + 1, cut]
        if keep_u is not None:
            keep_u[:, cut] = u.astype(bf16)
        z, phi = gelu(u)
        z = z.astype(bf16)
        if keep_gelu is not None:
            keep_gelu[0][step, :, cut] = z
            keep_gelu[1][:, cut] = gelu_slope(u, phi).astype(bf16)
        y = y + mm(z, w2[cut, :])
    return y


def backward(step, block, x, mid, dy, refs, slope, tick=lambda point: None):
    (gain, wqkv, wp, w1, w2, xs, qw, pr, dos, dss, dm_all, du_all, da_all, dp_all, small, dbias) = refs

    def add_small(row, value):
        small[row : row + 1, :] += value

    dm = dy.astype(bf16)
    dm_all[step] = dm
    add_small(7, jnp.sum(dm.astype(f32), 0, keepdims=True))
    dn2 = jnp.zeros((ROWS, D), f32)
    for part in range(4):
        cut = slice(384 * part, 384 * (part + 1))
        du = (mm_bt(dm, w2[cut, :]) * slope(cut)).astype(bf16)
        du_all[step, :, cut] = du
        add_small(8 + part, jnp.sum(du.astype(f32), 0, keepdims=True))
        dn2 = dn2 + mm_bt(du, w1[:, cut])
        if part % 2:
            tick(1 + part // 2)
    xh2, rstd2 = norm(mid)
    dx2, dgain, dbeta = norm_back(xh2, rstd2, dn2, gain[block, 1:2, :])
    add_small(1, dgain)
    add_small(3, dbeta)
    dmid = dy + dx2
    da = dmid.astype(bf16)
    da_all[step] = da
    add_small(6, jnp.sum(da.astype(f32), 0, keepdims=True))
    do = mm_bt(da, wp[...])
    for g in range(GROUPS):
        to_windows(dos, g, do[:, LANES * g : LANES * (g + 1)])

    tick(3)

    def probs_back(w, carry):
        cg, c = w // 8, w % 8
        for g in range(GROUPS):
            d = spread(dos[cg, g, pl.ds(c, SLOT, stride=8), :].astype(bf16))
            p16 = pr[w, g]
            p = p16.astype(f32)
            t = p * mm_bt(qw[w, 2 * GROUPS + g][:KEYS], d)
            ds = (t - p * jnp.sum(t, 0, keepdims=True)).astype(bf16)
            dss[w, g] = ds
            dbias[g] += ds.astype(f32)
            xs[cg, 2 * GROUPS + g, pl.ds(c, KEYS, stride=8), :] = mm(p16, d)
        return carry

    lax.fori_loop(0, HALF, probs_back, 0, unroll=2)

    tick(4)

    def scores_back(w, carry):
        cg, c = w // 8, w % 8
        for g in range(GROUPS):
            ds = dss[w, g]
            dk = mm(ds, spread(qw[w, g])) * (1.0 / LOG2E)
            dq = gather_heads(mm_at(ds, qw[w, GROUPS + g][:KEYS])) * SCALE
            xs[cg, g, pl.ds(c, KEYS, stride=8), :] = dq
            xs[cg, GROUPS + g, pl.ds(c, KEYS, stride=8), :] = dk
        return carry

    lax.fori_loop(0, HALF, scores_back, 0)
    tick(5)
    for n in range(3 * GROUPS):
        dp_all[step, :, LANES * n : LANES * (n + 1)] = from_windows(xs, n).astype(bf16)
    dp = dp_all[step]
    add_small(4, jnp.sum(dp[:, :D].astype(f32), 0, keepdims=True))
    add_small(5, jnp.sum(dp[:, 2 * D :].astype(f32), 0, keepdims=True))
    dn1 = mm_bt(dp, wqkv[...])
    tick(6)
    xh1, rstd1 = norm(x)
    dx1, dgain, dbeta = norm_back(xh1, rstd1, dn1, gain[block, 0:1, :])
    add_small(0, dgain)
    add_small(2, dbeta)
    return dmid + dx1


def weight_grads(n1, n2, o16, z, dm, du, da, dp, out):
    rows = 2 * ROWS

    def flat(ref, cut=slice(None)):
        return ref[:, :, cut].reshape(rows, -1)

    for j in range(2):
        up = mm_at(flat(n2), flat(du, slice(768 * j, 768 * (j + 1)))).astype(bf16)
        out[2 * D * j : 2 * D * j + D, :] = up[:, :D]
        out[2 * D * j + D : 2 * D * (j + 1), :] = up[:, D:]
    for j in range(3):
        out[4 * D + 512 * j : 4 * D + 512 * (j + 1), :] = mm_at(
            flat(z, slice(512 * j, 512 * (j + 1))), flat(dm)
        ).astype(bf16)
    qkv = mm_at(flat(n1), flat(dp)).astype(bf16)
    for j in range(3):
        out[D * (8 + j) : D * (9 + j), :] = qkv[:, D * j : D * (j + 1)]
    out[11 * D : 12 * D, :] = mm_at(flat(o16), flat(da)).astype(bf16)


def first_kernel(
    ext, x_ref, gain, beta, wqkv, qvb, bias, wp, ob, w1, b1, w2,
    y_ref, qw, pr, o16, mid, u_ref, xs, ss, os,
):
    step = pl.program_id(0)

    @pl.when(step == 0)
    def _():
        xs[...] = jnp.zeros_like(xs)

    x = x_ref[...].reshape(ROWS, D).astype(f32)
    y = forward(
        step, 0, False, x, (ext, gain, beta, wqkv, qvb, bias, wp, ob, w1, b1, w2, xs, qw, ss, pr, os, o16, mid), keep_u=u_ref
    )
    y_ref[...] = y.astype(bf16).reshape(y_ref.shape)


def second_kernel(
    ext, count, x_ref, cot_ref, gain, beta, wqkv, qvb, bias, wp, ob, w1, b1, w2,
    y_ref, dx_ref, grads, small, dbias,
    xs, qw, ss, pr, os, mid, slope, dos, dss, n1, n2, o16, z, dm, du, da, dp,
):
    step = pl.program_id(0)

    @pl.when(step == 0)
    def _():
        xs[...] = jnp.zeros_like(xs)
        dos[...] = jnp.zeros_like(dos)
        small[...] = jnp.zeros_like(small)
        dbias[...] = jnp.zeros_like(dbias)

    x = x_ref[...].reshape(ROWS, D).astype(f32)
    live = lax.broadcasted_iota(jnp.int32, (CELLS, HALF, 1), 1) + step * HALF < count[0]
    y = forward(
        step, 1, True, x,
        (ext, gain, beta, wqkv, qvb, bias, wp, ob, w1, b1, w2, xs, qw, ss, pr, os, o16.at[step], mid),
        n1, n2, (z, slope),
    )
    y_ref[...] = jnp.where(live, y.reshape(CELLS, HALF, D), 0.0).astype(bf16)
    dy = jnp.where(live, cot_ref[...].astype(f32), 0.0).reshape(ROWS, D)
    dx = backward(
        step, 1, x, mid[...], dy,
        (gain, wqkv, wp, w1, w2, xs, qw, pr, dos, dss, dm, du, da, dp, small, dbias),
        lambda cut: slope[:, cut].astype(f32),
    )
    dx_ref[...] = dx.astype(bf16).reshape(dx_ref.shape)

    @pl.when(step == 1)
    def _():
        weight_grads(n1, n2, o16, z, dm, du, da, dp, grads)


def third_kernel(
    x_ref, dy_ref, qw, pr, o_ref, mid, u_ref, gain, beta, wqkv, wp, w1, w2, other_ref,
    dx_ref, grads, small, dbias, other_out,
    xs, dos, dss, n1, n2, o16, z, dm, du, da, dp, other_sum, landing, send, recv, free, local, loads,
):
    step = pl.program_id(0)
    exchange = Exchange(other_sum, landing, send, recv, free)
    ticks = 7

    def kept(half):
        rows = pl.ds(half * ROWS, ROWS)
        return (
            pltpu.make_async_copy(u_ref.at[rows], z.at[half], loads.at[0, half]),
            pltpu.make_async_copy(o_ref.at[rows], o16.at[half], loads.at[1, half]),
        )

    def tick(point):
        for s in range(2):
            @pl.when(step == s)
            def _():
                exchange.advance(s * ticks + point)

    @pl.when(step == 0)
    def _():
        exchange.greet()
        load = pltpu.make_async_copy(other_ref, other_sum, local)
        load.start()
        for half in range(2):
            for copy in kept(half):
                copy.start()
        load.wait()

    @pl.when(step == 0)
    def _():
        xs[...] = jnp.zeros_like(xs)
        dos[...] = jnp.zeros_like(dos)
        small[...] = jnp.zeros_like(small)
        dbias[...] = jnp.zeros_like(dbias)

    tick(0)
    for half in range(2):
        @pl.when(step == half)
        def _():
            for copy in kept(half):
                copy.wait()

    x = x_ref[...].reshape(ROWS, D).astype(f32)
    xh, _ = norm(x)
    n1[step] = (xh * gain[0, 0:1, :] + beta[0, 0:1, :]).astype(bf16)
    middle = mid[...]
    xh2, _ = norm(middle)
    n2[step] = (xh2 * gain[0, 1:2, :] + beta[0, 1:2, :]).astype(bf16)

    def slope(cut):
        u = z[step, :, cut].astype(f32)
        value, phi = gelu(u)
        z[step, :, cut] = value.astype(bf16)
        return gelu_slope(u, phi)

    dx = backward(
        step, 0, x, middle, dy_ref[...].astype(f32).reshape(ROWS, D),
        (gain, wqkv, wp, w1, w2, xs, qw, pr, dos, dss, dm, du, da, dp, small, dbias),
        slope,
        tick,
    )
    dx_ref[...] = dx.astype(bf16).reshape(dx_ref.shape)

    @pl.when(step == 1)
    def _():
        weight_grads(n1, n2, o16, z, dm, du, da, dp, grads)
        for k in range(2 * ticks, exchange.stages + 1):
            exchange.advance(k)
        store = pltpu.make_async_copy(other_sum, other_out, local)
        store.start()
        store.wait()


def whole(shape):
    return pl.BlockSpec(shape, lambda s: (0,) * len(shape), pipeline_mode=pl.Buffered(1))


def of_block(block, *shape):
    return pl.BlockSpec((None,) + shape, lambda s: (block,) + (0,) * len(shape), pipeline_mode=pl.Buffered(1))


def by_half(*shape, buffers=2):
    return pl.BlockSpec(shape, lambda s: (s,) + (0,) * (len(shape) - 1), pipeline_mode=pl.Buffered(buffers))


ANY_SPEC = pl.BlockSpec(memory_space=pl.ANY)
SMEM_SPEC = pl.BlockSpec(memory_space=pltpu.SMEM)
TOKEN_SPEC = pl.BlockSpec((CELLS, HALF, D), lambda s: (0, s, 0))
XS = VMEM((2, 3 * GROUPS, 8 * SLOT, LANES), f32)
DOS = VMEM((2, GROUPS, 8 * SLOT, LANES), f32)
QW = (HALF, 3 * GROUPS, SLOT, LANES)
PR = (HALF, GROUPS, KEYS, 4 * SLOT)
OPERANDS = [VMEM((2, ROWS, width), bf16) for width in (D, D, D, FF, D, FF, D, 3 * D)]


def params():
    return pltpu.CompilerParams(vmem_limit_bytes=61 * 2**20, dimension_semantics=("arbitrary",))


def run_first(ext, x, gain, beta, wqkv, qvb, bias, wp, ob, w1, b1, w2):
    crops = x.shape[1]
    return pl.pallas_call(
        first_kernel,
        grid=(2,),
        out_shape=(
            jax.ShapeDtypeStruct(x.shape, bf16),
            jax.ShapeDtypeStruct((crops,) + QW[1:], bf16),
            jax.ShapeDtypeStruct((crops,) + PR[1:], bf16),
            jax.ShapeDtypeStruct((2 * ROWS, D), bf16),
            jax.ShapeDtypeStruct((2 * ROWS, D), f32),
            jax.ShapeDtypeStruct((2 * ROWS, FF), bf16),
        ),
        in_specs=[
            SMEM_SPEC, TOKEN_SPEC, whole(gain.shape), whole(beta.shape), of_block(0, D, 3 * D), whole(qvb.shape),
            of_block(0, GROUPS, KEYS, 4 * SLOT), of_block(0, D, D), whole(ob.shape), of_block(0, D, FF),
            whole(b1.shape), of_block(0, FF, D),
        ],
        out_specs=(TOKEN_SPEC, by_half(*QW), by_half(*PR), by_half(ROWS, D), by_half(ROWS, D), by_half(ROWS, FF)),
        scratch_shapes=[XS, VMEM(PR, f32), VMEM((2, GROUPS, 8 * KEYS, LANES), f32)],
        compiler_params=params(),
        name="first_forward",
    )(ext, x, gain, beta, wqkv, qvb, bias, wp, ob, w1, b1, w2)


GRAD_SHAPES = (
    jax.ShapeDtypeStruct((SLABS * D, D), bf16),
    jax.ShapeDtypeStruct((16, D), f32),
    jax.ShapeDtypeStruct((GROUPS, KEYS, 4 * SLOT), f32),
)
GRAD_SPECS = (whole((SLABS * D, D)), whole((16, D)), whole((GROUPS, KEYS, 4 * SLOT)))


def run_second(ext, count, x, cot, gain, beta, wqkv, qvb, bias, wp, ob, w1, b1, w2):
    return pl.pallas_call(
        second_kernel,
        grid=(2,),
        out_shape=(jax.ShapeDtypeStruct(x.shape, bf16), jax.ShapeDtypeStruct(x.shape, bf16)) + GRAD_SHAPES,
        in_specs=[
            SMEM_SPEC, SMEM_SPEC, TOKEN_SPEC, TOKEN_SPEC, whole(gain.shape), whole(beta.shape), of_block(1, D, 3 * D),
            whole(qvb.shape), of_block(1, GROUPS, KEYS, 4 * SLOT), of_block(1, D, D), whole(ob.shape),
            of_block(1, D, FF), whole(b1.shape), of_block(1, FF, D),
        ],
        out_specs=(TOKEN_SPEC, TOKEN_SPEC) + GRAD_SPECS,
        scratch_shapes=[
            XS, VMEM(QW, bf16), VMEM(PR, f32), VMEM(PR, bf16), VMEM((2, GROUPS, 8 * KEYS, LANES), f32),
            VMEM((ROWS, D), f32), VMEM((ROWS, FF), bf16), DOS, VMEM(PR, bf16),
        ] + OPERANDS,
        compiler_params=params(),
        name="second_block",
    )(ext, count, x, cot, gain, beta, wqkv, qvb, bias, wp, ob, w1, b1, w2)


def run_third(x, dy, qw, pr, o16, mid, u, gain, beta, wqkv, wp, w1, w2, other):
    return pl.pallas_call(
        third_kernel,
        grid=(2,),
        out_shape=(jax.ShapeDtypeStruct(x.shape, bf16),) + GRAD_SHAPES + GRAD_SHAPES[:1],
        in_specs=[
            TOKEN_SPEC, TOKEN_SPEC, by_half(*QW), by_half(*PR, buffers=1), ANY_SPEC, by_half(ROWS, D), ANY_SPEC,
            whole(gain.shape), whole(beta.shape), of_block(0, D, 3 * D), of_block(0, D, D), of_block(0, D, FF),
            of_block(0, FF, D), ANY_SPEC,
        ],
        out_specs=(TOKEN_SPEC,) + GRAD_SPECS + (ANY_SPEC,),
        scratch_shapes=[XS, DOS, VMEM(PR, bf16)] + OPERANDS + [VMEM((SLABS * D, D), bf16)] + exchange_scratch() + [
            pltpu.SemaphoreType.DMA(()), pltpu.SemaphoreType.DMA((2, 2)),
        ],
        compiler_params=pltpu.CompilerParams(
            vmem_limit_bytes=63 * 2**20, dimension_semantics=("arbitrary",), collective_id=0, has_side_effects=True
        ),
        name="first_backward",
    )(x, dy, qw, pr, o16, mid, u, gain, beta, wqkv, wp, w1, w2, other)


def partner(value, apart):
    pairs = [(source, source ^ 2**apart) for source in range(lax.axis_size("win"))]
    return lax.ppermute(value, "win", pairs)


def shift_in(cells_here):
    grid = cells_here.reshape((WINDOW, WINDOW) + cells_here.shape[1:])
    widened = jnp.concatenate([grid[:, SHIFT:], partner(grid[:, :SHIFT], 0)], 1)
    return jnp.concatenate([widened[SHIFT:], partner(widened[:SHIFT], 1)], 0).reshape(cells_here.shape)


def shift_out(cells_here):
    keep = WINDOW - SHIFT
    grid = cells_here.reshape((WINDOW, WINDOW) + cells_here.shape[1:])
    widened = jnp.concatenate([partner(grid[:, keep:], 0), grid[:, :keep]], 1)
    return jnp.concatenate([partner(widened[keep:], 1), widened[:keep]], 0).reshape(cells_here.shape)


def orders():
    n_img, n_win = lax.axis_size("img"), lax.axis_size("win")
    core = [("win", 0)]
    across = [("win", b) for b in range(1, n_win.bit_length() - 1)]
    img = [("img", b) for b in range(n_img.bit_length() - 1)]
    return [core + across + img, core + img[:1] + across + img[1:], core + img[1:] + across + img[:1]]


class Exchange:
    def __init__(self, buf, landing, send, recv, free):
        self.buf, self.landing, self.send, self.recv, self.free = buf, landing, send, recv, free
        chains = orders()
        self.bits = len(chains[0])
        self.stages = 2 * self.bits
        self.index = {axis: lax.axis_index(axis) for axis in ("img", "win")}
        rows = buf.shape[0] // len(chains)
        self.plans, land = [], 0
        for c, chain in enumerate(chains):
            start, size, plan = c * rows, rows, []
            for axis, bit in chain:
                mine = (self.index[axis] // 2**bit) % 2
                halve = size % 32 == 0
                if halve:
                    size = size // 2
                keep, give = (start + mine * size, start + (1 - mine) * size) if halve else (start, start)
                to = {axis: self.index[axis] + 2**bit - 2 ** (bit + 1) * mine}
                plan.append((keep, give, size, land, halve, to))
                start, land = keep, land + size
            self.plans.append(plan)

    def greet(self):
        barrier = pltpu.get_barrier_semaphore()
        for plan in self.plans[:1]:
            for *_, to in plan:
                pl.semaphore_signal(barrier, inc=1, device_id=to, device_id_type=MESH)
            pl.semaphore_wait(barrier, len(plan))

    def copy(self, c, k):
        n = min(k, self.stages - 1 - k)
        keep, give, size, land, halve, to = self.plans[c][n]
        if k >= self.bits and not halve:
            return None
        if k < self.bits:
            source, target = self.buf.at[pl.ds(pl.multiple_of(give, 16), size)], self.landing.at[pl.ds(land, size)]
        else:
            source = target = self.buf.at[pl.ds(pl.multiple_of(keep, 16), size)]
        return pltpu.make_async_remote_copy(
            source, target, self.send.at[c, k], self.recv.at[c, k], device_id=to, device_id_type=MESH
        )

    def start(self, k):
        for c in range(len(self.plans)):
            copy = self.copy(c, k)
            if copy is not None:
                if k >= self.bits:
                    pl.semaphore_wait(self.free.at[c, self.stages - 1 - k], 1)
                copy.start()

    def finish(self, k):
        for c in range(len(self.plans)):
            copy = self.copy(c, k)
            if copy is None:
                continue
            copy.wait()
            if k >= self.bits:
                continue
            keep, _, size, land, halve, to = self.plans[c][k]
            if halve:
                pl.semaphore_signal(self.free.at[c, k], inc=1, device_id=to, device_id_type=MESH)
            tile = 96 if size % 96 == 0 else 16

            def add(i, carry, keep=keep, land=land, tile=tile):
                here = pl.ds(pl.multiple_of(keep + i * tile, 16), tile)
                there = pl.ds(pl.multiple_of(land + i * tile, 16), tile)
                self.buf[here, :] = (self.buf[here, :].astype(f32) + self.landing[there, :].astype(f32)).astype(bf16)
                return carry

            lax.fori_loop(0, size // tile, add, 0)

    def advance(self, k):
        if 1 <= k <= self.stages:
            self.finish(k - 1)
        if k < self.stages:
            self.start(k)


def exchange_scratch():
    landing = 0
    for chain in orders():
        size = SLABS * D // 3
        for _ in chain:
            size = size // 2 if size % 32 == 0 else size
            landing += size
    stages = 2 * len(orders()[0])
    dma = pltpu.SemaphoreType.DMA((3, stages))
    return [VMEM((landing, D), bf16), dma, dma, pltpu.SemaphoreType.REGULAR((3, stages // 2))]


def sum_kernel(g_ref, s_ref, out, s_out, landing, send, recv, free, s_land, s_send, s_recv):
    exchange = Exchange(out, landing, send, recv, free)
    exchange.greet()
    out[...] = g_ref[...]
    s_out[...] = s_ref[...]
    exchange.start(0)
    for n, (*_, to) in enumerate(exchange.plans[0]):
        small = pltpu.make_async_remote_copy(
            s_out, s_land.at[n], s_send.at[n], s_recv.at[n], device_id=to, device_id_type=MESH
        )
        small.start()
        exchange.advance(n + 1)
        small.wait()
        s_out[...] += s_land[n]
    for k in range(exchange.bits + 1, exchange.stages + 1):
        exchange.advance(k)


def sum_all(grads, small):
    bits = len(orders()[0])
    return pl.pallas_call(
        sum_kernel,
        out_shape=(jax.ShapeDtypeStruct(grads.shape, bf16), jax.ShapeDtypeStruct(small.shape, f32)),
        in_specs=[pl.BlockSpec(memory_space=VMEM)] * 2,
        out_specs=(pl.BlockSpec(memory_space=VMEM),) * 2,
        scratch_shapes=exchange_scratch() + [
            VMEM((bits,) + small.shape, f32), pltpu.SemaphoreType.DMA((bits,)), pltpu.SemaphoreType.DMA((bits,)),
        ],
        compiler_params=pltpu.CompilerParams(
            collective_id=1, has_side_effects=True, vmem_limit_bytes=30 * 2**20
        ),
        name="sum_gradients",
    )(grads, small)


def finish_kernel(*refs):
    ins, outs = refs[:8], refs[8:]
    for n, out in enumerate(outs):
        for block in range(2):
            out[block] = ins[2 * n + block][...].astype(f32)


def finish(grads_one, grads_two):
    slabs = [lambda j: (j, 0), lambda j: (4 + j, 0), lambda j: (8 + jnp.minimum(j, 2), 0), lambda j: (11, 0)]
    targets = [lambda j: (0, 0, j), lambda j: (0, j, 0), lambda j: (0, 0, jnp.minimum(j, 2)), lambda j: (0, 0, 0)]
    return pl.pallas_call(
        finish_kernel,
        grid=(4,),
        out_shape=tuple(jax.ShapeDtypeStruct((2,) + s, f32) for s in ((D, FF), (FF, D), (D, 3 * D), (D, D))),
        in_specs=[pl.BlockSpec((D, D), index) for index in slabs for _ in range(2)],
        out_specs=tuple(pl.BlockSpec((2, D, D), index) for index in targets),
        compiler_params=params(),
        name="finish_gradients",
    )(*[grads_one, grads_two] * 4)


def position_lookup():
    j = jnp.arange(KEYS)[:, None]
    i = jnp.arange(SLOT)[None, :]
    side = SIDE - 1
    index = (i // WINDOW - j // WINDOW + WINDOW - 1) * side + i % WINDOW - j % WINDOW + WINDOW - 1
    index = jnp.where((i < CELLS) & (j < CELLS), index, -1).reshape(-1)
    return (jnp.arange(side * side)[:, None] == index[None, :]).astype(f32)


def on_device(
    tokens, cotangent, crop_counts, crop_extent, norm_gain, norm_bias, qkv_weight, qv_bias, rel_table, proj_weight,
    out_bias, fc1_weight, fc1_bias, fc2_weight,
):
    crops = tokens.shape[0]
    x = tokens.reshape(crops, CELLS, D).transpose(1, 0, 2)
    cot = cotangent.reshape(crops, CELLS, D).transpose(1, 0, 2)
    lookup = position_lookup()
    highest = lax.Precision.HIGHEST
    bias = jnp.einsum("bkh,kp->bhp", rel_table, lookup, precision=highest) * LOG2E
    bias = bias.reshape(2, GROUPS, 4, KEYS, SLOT).transpose(0, 1, 3, 2, 4)
    bias = jnp.where(jnp.arange(KEYS)[:, None, None] < CELLS, bias, NEG).reshape(2, GROUPS, KEYS, 4 * SLOT)

    cot_shifted = shift_in(cot)
    x1, qw, pr, o16, mid, u = run_first(
        crop_extent, x, norm_gain, norm_bias, qkv_weight, qv_bias, bias, proj_weight, out_bias, fc1_weight, fc1_bias,
        fc2_weight,
    )
    x1 = shift_in(x1)
    y2, dr, grads_two, small_two, dbias_two = run_second(
        crop_extent, crop_counts, x1, cot_shifted, norm_gain, norm_bias, qkv_weight, qv_bias, bias, proj_weight,
        out_bias, fc1_weight, fc1_bias, fc2_weight,
    )
    output = shift_out(y2)
    dx1 = shift_out(dr)
    dx, grads_one, small_one, dbias_one, sum_two = run_third(
        x, dx1, qw, pr, o16, mid, u, norm_gain, norm_bias, qkv_weight, proj_weight, fc1_weight, fc2_weight, grads_two
    )
    dbias = jnp.stack([dbias_one, dbias_two]).reshape(2, GROUPS, KEYS, 4, SLOT).transpose(0, 1, 3, 2, 4)
    table = jnp.einsum("hp,kp->hk", dbias.reshape(2 * HEADS, KEYS * SLOT), lookup, precision=highest)
    table = jnp.pad(table, ((0, 0), (0, D - table.shape[1])))
    small = jnp.concatenate([small_one, small_two, table], 0)
    sum_one, small = sum_all(grads_one, small)

    fc1, fc2, qkv, proj = finish(sum_one, sum_two)
    rows = small[:32].reshape(2, 16, D)
    table = small[32:, : rel_table.shape[1]].reshape(2, HEADS, -1).transpose(0, 2, 1)
    back = lambda v: v.transpose(1, 0, 2).reshape(tokens.shape)
    return (
        back(output), back(dx), rows[:, 0:2], rows[:, 2:4], qkv, rows[:, 4:6], table, proj, rows[:, 6:8], fc1,
        rows[:, 8:12].reshape(2, FF), fc2,
    )


def solution(mesh):
    split = P("img", "win", None, None)
    return jax.shard_map(
        on_device,
        mesh=mesh,
        in_specs=(split, split, P("img"), P("img", None)) + (P(),) * 10,
        out_specs=(split, split) + (P(),) * 10,
        check_vma=False,
    )
```

time: 889 us -> 343 us (0.39)
  Pallas kernels: 0 us -> 267 us
  matrix products: 270 us -> 3.36 us
  local copies, waits for them, and re-layouts: 275 us -> 18 us
  waiting for transfers between devices: 178 us -> 32.5 us
  other arithmetic: 91.9 us -> 11.9 us
  blocking collectives: 44.1 us -> 0 us
  between operations: 17.1 us -> 1.84 us
    pallas_call x0 -> x5, Pallas kernels: none -> 267 us  [the longest x1 87.6 us: run_third(): pl.pallas_call(third_kernel, grid=(2,), out_shape=(jax.ShapeDtypeStruct(x...]
    dot_general x40 -> x2, matrix products: 270 us -> 3.36 us  [the longest x1 2.24 us: on_device(): jnp.einsum('hp,kp->hk', dbias.reshape(2 * HEADS, KEYS * SLOT), lookup, pr...]
    psum x1 -> x0, waiting for transfers between devices: 147 us -> none  [on_device(): lax.psum((stacked[0], stacked[1], stacked[2], stacked[3], stacked[4], sta...]
    reshape x27 -> x4, local copies, waits for them, and re-layouts: 146 us -> 3.58 us  [the longest x1 2.02 us: on_device(): dbias.reshape(2 * HEADS, KEYS * SLOT)]
    convert_element_type x20 -> x0, local copies, waits for them, and re-layouts: 64 us -> none  [the longest x2 11.2 us: block_backward(): grad_queries = (jnp.einsum('chij,cjhe->cihe', grad_scores, keys_low, pref...]
    psum x1 -> x0, blocking collectives: 44.1 us -> none  [on_device(): lax.psum((stacked[0], stacked[1], stacked[2], stacked[3], stacked[4], sta...]
    reduce_sum x16 -> x0, other arithmetic: 32.7 us -> none  [the longest x2 19.4 us: block_backward(): grad_bias_heads = jnp.sum(grad_scores, 0, dtype=jnp.float32)]
    sub x3 -> x0, other arithmetic: 26 us -> none  [the longest x2 25.9 us: block_parts(): exp_terms = jnp.exp(scores - row_top)]
  transfers between devices with their start and end apart: 9 -> 8, of which waited for: 5 -> 4; matrix products, arithmetic and copies ran while one was open for 24% -> 6% of each run, Pallas kernels for 0% -> 46%
where the time goes in v1:
time: 343 us; the launch traced here: 341 us
  Pallas kernels  267 us (78%)
  waiting for transfers between devices  32.5 us (9%)
  local copies, waits for them, and re-layouts  18 us (5%)
  other arithmetic  11.9 us (3%)
  starting transfers between devices  6.78 us (2%)
    pallas_call x1, Pallas kernels, run_third(): pl.pallas_call(third_kernel, grid=(2,), out_shape=(jax.ShapeDtypeStruct(x...  87.6 us
    pallas_call x1, Pallas kernels, run_second(): pl.pallas_call(second_kernel, grid=(2,), out_shape=(jax.ShapeDtypeStruct(...  77.6 us
    pallas_call x1, Pallas kernels, sum_all(): pl.pallas_call(sum_kernel, out_shape=(jax.ShapeDtypeStruct(grads.shape, b...  61.1 us
    ppermute x8, waiting for transfers between devices, partner(): return lax.ppermute(value, 'win', pairs)  32.5 us
    pallas_call x1, Pallas kernels, run_first(): pl.pallas_call(first_kernel, grid=(2,), out_shape=(jax.ShapeDtypeStruct(x...  32.3 us
    pallas_call x1, Pallas kernels, finish(): pl.pallas_call(finish_kernel, grid=(4,), out_shape=tuple((jax.ShapeDtypeS...  8.53 us
  transfers between devices with their start and end apart: 8, of which 4 were waited for; matrix products, arithmetic and copies ran while one was open for 6% of the time, Pallas kernels for 46%

profile of v1, /device:TPU:0, one launch (start us, length us, event | category | flops | bytes accessed | tf_op | source)
XLA Modules:
  0.0 341.4 jit_solution(7850481097732318785)
XLA Ops:
  3.6 1.2 reshape.220.bias
  5.5 32.3 %first_forward.1 = (bf16[49,32,384]{2,1,0:T(8,128)(2,1)}, bf16[32,9,64,128]{3,2,1,0:T(8,128)(2,1)}, bf16[32,3,56,256]{3,2,1,0:T(8,128)(2,1)}, bf16[1568,384]{1,0...) custom-call(s32[32,2]{1,0:T(8,128)} %copy.35.ext, bf16[49,32,384]{2,1,0:T(8,128)(2,1)} %bitcast.42, ...), custom_call_target="tpu_custom_call" | custom-call | tf_op jit(solution)/shard_map/first_forward/pallas_call | solution.py:440
  37.8 1.2 slice.93
  39.8 1.2 collective-permute-done
  41.1 2.9 collective-permute-start.1
  45.6 11.0 %collective-permute-done.1 = bf16[3,7,32,384]{3,2,1,0:T(8,128)(2,1)S(1)} collective-permute-done((bf16[3,7,32,384]{3,2,1,0:T(8,128)(2,1)S(1)}, bf16[3,7,32,384]{3,2,1,0:T(8,128)(2,1)S(1)}, u32[]{:S(2)}, u32[]{:S(2)}) %collective-permute-start.1) | collective-permute-done | bytes 516128 | tf_op jit(solution)/shard_map/ppermute | solution.py:514
  56.5 1.2 pad_maximum_fusion.2
  57.7 9.4 %collective-permute-done.3 = bf16[3,7,32,384]{3,2,1,0:T(8,128)(2,1)S(1)} collective-permute-done((bf16[3,7,32,384]{3,2,1,0:T(8,128)(2,1)S(1)}, bf16[3,7,32,384]{3,2,1,0:T(8,128)(2,1)S(1)}, u32[]{:S(2)}, u32[]{:S(2)}) %collective-permute-start.3) | collective-permute-done | bytes 516128 | tf_op jit(solution)/shard_map/ppermute | solution.py:514
  67.1 1.2 pad_maximum_fusion.3
  68.3 77.6 %second_block.1 = (bf16[49,32,384]{2,1,0:T(8,128)(2,1)}, bf16[49,32,384]{2,1,0:T(8,128)(2,1)}, bf16[4608,384]{1,0:T(8,128)(2,1)}, f32[16,384]{1,0:T(8,128)}, f32[3,56,256]{2,1,0:T(8,128)}) custom-call(s32[32,2]{1,0:T(8,128)} %copy.35.ext, s32[1]{0:T(128)S(6)} %copy.43.count, bf16[49,32,384]{2,1,0:T(8,128)(2,1)} %bitcast.44, bf16[49,32,384]{2,1,0:T(8,128)(2,1)} %bitcast.45, ...), custom_call_target="tpu_custom_call" | custom-call | tf_op jit(solution)/shard_map/second_block/pallas_call | solution.py:472
  145.9 1.2 slice.102
  147.2 1.2 slice.103
  149.9 1.7 collective-permute-start.7
  154.0 10.8 %collective-permute-done.7 = bf16[3,7,32,384]{3,2,1,0:T(8,128)(2,1)} collective-permute-done((bf16[3,7,32,384]{3,2,1,0:T(8,128)(2,1)}, bf16[3,7,32,384]{3,2,1,0:T(8,128)(2,1)}, u32[]{:S(2)}, u32[]{:S(2)}) %collective-permute-start.7) | collective-permute-done | bytes 516128 | tf_op jit(solution)/shard_map/ppermute | solution.py:514
  164.8 2.2 fusion.6
  167.0 87.6 %first_backward.1 = (bf16[49,32,384]{2,1,0:T(8,128)(2,1)}, bf16[4608,384]{1,0:T(8,128)(2,1)}, f32[16,384]{1,0:T(8,128)}, f32[3,56,256]{2,1,0:T(8,128)}, bf16[4608,384]{1,0:T(8,128)(2,1)}) custom-call(bf16[49,32,384]{2,1,0:T(8,128)(2,1)} %bitcast.43, bf16[49,32,384]{2,1,0:T(8,128)(2,1)} %bitcast.41, bf16[32,9,64,128]{3,2,1,0:T(8,128)(2,1)} %get-tuple-element.37.qw, ...), custom_call_target="tpu_custom_call" | custom-call | tf_op jit(solution)/shard_map/first_backward/pallas_call | solution.py:492
  254.6 1.8 stack.9
  257.6 1.9 maximum_bitcast_fusion
  259.5 2.0 reshape.232
  261.5 2.2 fusion.1
  264.5 61.1 %sum_gradients.1 = (bf16[4608,384]{1,0:T(8,128)(2,1)S(1)}, f32[56,384]{1,0:T(8,128)S(1)}) custom-call(bf16[4608,384]{1,0:T(8,128)(2,1)S(1)} %copy-done.3, f32[56,384]{1,0:T(8,128)S(1)} %select_maximum_fusion.s_ref), custom_call_target="tpu_custom_call" | custom-call | tf_op jit(solution)/shard_map/sum_gradients/pallas_call | solution.py:648
  325.7 1.7 copy-done.2
  328.7 8.5 %finish_gradients.1 = (f32[2,384,1536]{2,1,0:T(8,128)}, f32[2,1536,384]{2,1,0:T(8,128)}, f32[2,384,1152]{2,1,0:T(8,128)}, f32[2,384,384]{2,1,0:T(8,128)}) custom-call(bf16[4608,384]{1,0:T(8,128)(2,1)} %copy-done.2, bf16[4608,384]{1,0:T(8,128)(2,1)} %get-tuple-element.51.refs_1_.refs_3_.refs_5_.refs_7_, bf16[4608,384]{1,0:T(8,128)(2,1)} %copy-done.2, ...), custom_call_target="tpu_custom_call" | custom-call | tf_op jit(solution)/shard_map/finish_gradients/pallas_call | solution.py:673
  337.8 2.3 fusion.7
  (72 shorter events, 14.1 us)
Async XLA Ops:
  0.6 0.7 copy-start
  3.3 1.4 copy-start.13
  5.5 34.0 %copy-start.8 = (bf16[32,1,49,384]{3,0,2,1:T(8,128)(2,1)S(1)}, bf16[32,1,49,384]{3,0,2,1:T(8,128)(2,1)}, u32[]{:S(2)}) copy-start(bf16[32,1,49,384]{3,0,2,1:T(8,128)(2,1)} %param.15) | copy-start | bytes 3612676
  37.8 1.9 copy-start.11
  39.0 2.0 collective-permute-start
  39.5 4.6 %collective-permute-start.2 = (bf16[7,3,32,384]{3,2,1,0:T(8,128)(2,1)S(1)}, bf16[7,3,32,384]{3,2,1,0:T(8,128)(2,1)S(1)}, u32[]{:S(2)}, u32[]{:S(2)}) collective-permute-start(bf16[7,3,32,384]{3,2,1,0:T(8,128)(2,1)S(1)} %slice.97), channel_id=1, source_target_pairs={{0,1},{1,0},{2,3},{3,2},{4,5},{5,4},{6,7},{7,6},{8,9},{9,8},{10,11... | collective-permute-start | bytes 1548296 | tf_op jit(solution)/shard_map/ppermute | solution.py:514
  41.1 15.5 %collective-permute-start.1 = (bf16[3,7,32,384]{3,2,1,0:T(8,128)(2,1)S(1)}, bf16[3,7,32,384]{3,2,1,0:T(8,128)(2,1)S(1)}, u32[]{:S(2)}, u32[]{:S(2)}) collective-permute-start(bf16[3,7,32,384]{3,2,1,0:T(8,128)(2,1)S(1)} %pad_maximum_fusion.7), channel_id=1, source_target_pairs={{0,2},{1,3},{2,0},{3,1},{4,6},{5,7},{6,4},{7,5},{8,10},{9,11},{10,... | collective-permute-start | bytes 1548296 | tf_op jit(solution)/shard_map/ppermute | solution.py:514
  44.2 22.9 %collective-permute-start.3 = (bf16[3,7,32,384]{3,2,1,0:T(8,128)(2,1)S(1)}, bf16[3,7,32,384]{3,2,1,0:T(8,128)(2,1)S(1)}, u32[]{:S(2)}, u32[]{:S(2)}) collective-permute-start(bf16[3,7,32,384]{3,2,1,0:T(8,128)(2,1)S(1)} %pad_maximum_fusion.6), channel_id=1, source_target_pairs={{0,2},{1,3},{2,0},{3,1},{4,6},{5,7},{6,4},{7,5},{8,10},{9,11},{10,... | collective-permute-start | bytes 1548296 | tf_op jit(solution)/shard_map/ppermute | solution.py:514
  145.9 2.5 copy-start.10
  147.1 2.0 collective-permute-start.6
  148.4 3.3 copy-start.12
  148.4 4.3 %collective-permute-start.4 = (bf16[7,3,32,384]{3,2,1,0:T(8,128)(2,1)S(1)}, bf16[7,3,32,384]{3,2,1,0:T(8,128)(2,1)S(1)}, u32[]{:S(2)}, u32[]{:S(2)}) collective-permute-start(bf16[7,3,32,384]{3,2,1,0:T(8,128)(2,1)S(1)} %slice.100), channel_id=1, source_target_pairs={{0,1},{1,0},{2,3},{3,2},{4,5},{5,4},{6,7},{7,6},{8,9},{9,8},{10,11... | collective-permute-start | bytes 1548296 | tf_op jit(solution)/shard_map/ppermute | solution.py:514
  149.9 14.9 %collective-permute-start.7 = (bf16[3,7,32,384]{3,2,1,0:T(8,128)(2,1)}, bf16[3,7,32,384]{3,2,1,0:T(8,128)(2,1)}, u32[]{:S(2)}, u32[]{:S(2)}) collective-permute-start(bf16[3,7,32,384]{3,2,1,0:T(8,128)(2,1)} %pad_maximum_fusion.4), channel_id=1, source_target_pairs={{0,2},{1,3},{2,0},{3,1},{4,6},{5,7},{6,4},{7,5},{8,10},{9,11},{10,... | collective-permute-start | bytes 1548296 | tf_op jit(solution)/shard_map/ppermute | solution.py:514
  151.7 2.0 copy-start.4
  152.8 14.2 %copy-start.6 = (bf16[7,3,32,384]{3,2,1,0:T(8,128)(2,1)}, bf16[7,3,32,384]{3,2,1,0:T(8,128)(2,1)S(1)}, u32[]{:S(2)}) copy-start(bf16[7,3,32,384]{3,2,1,0:T(8,128)(2,1)S(1)} %collective-permute-done.4) | copy-start | bytes 1548292
  153.7 184.1 %collective-permute-start.5 = (bf16[3,7,32,384]{3,2,1,0:T(8,128)(2,1)}, bf16[3,7,32,384]{3,2,1,0:T(8,128)(2,1)}, u32[]{:S(2)}, u32[]{:S(2)}) collective-permute-start(bf16[3,7,32,384]{3,2,1,0:T(8,128)(2,1)} %pad_maximum_fusion.5), channel_id=1, source_target_pairs={{0,2},{1,3},{2,0},{3,1},{4,6},{5,7},{6,4},{7,5},{8,10},{9,11},{10,... | collective-permute-start | bytes 1548296 | tf_op jit(solution)/shard_map/ppermute | solution.py:514
  256.4 8.1 %copy-start.3 = (bf16[4608,384]{1,0:T(8,128)(2,1)S(1)}, bf16[4608,384]{1,0:T(8,128)(2,1)}, u32[]{:S(2)}) copy-start(bf16[4608,384]{1,0:T(8,128)(2,1)} %get-tuple-element.44.g_ref) | copy-start | bytes 10616836
  325.7 1.7 copy-start.2
  328.7 9.2 %copy-start.5 = (bf16[7,4,32,384]{3,2,1,0:T(8,128)(2,1)S(1)}, bf16[7,4,32,384]{3,2,1,0:T(8,128)(2,1)}, u32[]{:S(2)}) copy-start(bf16[7,4,32,384]{3,2,1,0:T(8,128)(2,1)} %copy-done.4) | copy-start | bytes 2064388
  328.7 9.2 %copy-start.7 = (bf16[7,3,32,384]{3,2,1,0:T(8,128)(2,1)S(1)}, bf16[7,3,32,384]{3,2,1,0:T(8,128)(2,1)}, u32[]{:S(2)}) copy-start(bf16[7,3,32,384]{3,2,1,0:T(8,128)(2,1)} %copy-done.6) | copy-start | bytes 1548292
  337.8 2.3 copy-start.9
  340.1 1.0 copy-start.1

commit v2 on v1

v2 whole, which is shorter than its diff:
```python
import jax
import jax.numpy as jnp
from jax import lax
from jax.experimental import pallas as pl
from jax.experimental.pallas import tpu as pltpu
from jax.sharding import PartitionSpec as P

D = 384
FF = 1536
HEADS = 12
HEAD_DIM = 32
WINDOW = 7
SHIFT = 3
CELLS = WINDOW * WINDOW
SIDE = 2 * WINDOW
HALF = 16
ROWS = CELLS * HALF
LANES = 128
GROUPS = 3
KEYS = 56
SLOT = 64
SLABS = 12
SMALL = 16
TABLE = GROUPS * KEYS
SUMS = SLABS * D + 256
GROUPED = ((0, 1), (2, 3), (4, 5, 6))
NEG = -1e30
LOG2E = 1.4426950408889634
SCALE = HEAD_DIM**-0.5
MESH = pl.DeviceIdType.MESH

bf16 = jnp.bfloat16
f32 = jnp.float32
VMEM = pltpu.VMEM


def mm(a, b):
    return lax.dot_general(a, b, (((1,), (0,)), ((), ())), preferred_element_type=f32)


def mm_bt(a, b):
    return lax.dot_general(a, b, (((1,), (1,)), ((), ())), preferred_element_type=f32)


def mm_at(a, b):
    return lax.dot_general(a, b, (((0,), (0,)), ((), ())), preferred_element_type=f32)


def norm(x):
    centred = x - jnp.mean(x, -1, keepdims=True)
    rstd = lax.rsqrt(jnp.mean(centred * centred, -1, keepdims=True) + 1e-5)
    return centred * rstd, rstd


def norm_back(xh, rstd, dn, gain):
    e = dn * gain
    mean_e = jnp.mean(e, -1, keepdims=True)
    mean_ex = jnp.mean(e * xh, -1, keepdims=True)
    dx = rstd * (e - mean_e - xh * mean_ex)
    return dx, jnp.sum(dn * xh, 0, keepdims=True), jnp.sum(dn, 0, keepdims=True)


def gelu(u):
    phi = 0.5 + 0.5 * lax.erf(u * 0.7071067811865476)
    return u * phi, phi


def gelu_slope(u, phi):
    return phi + u * jnp.exp2(u * u * (-0.5 * LOG2E)) * 0.3989422804014327


def spread(rows):
    head = lax.broadcasted_iota(jnp.int32, rows.shape, 1) // HEAD_DIM
    zero = jnp.zeros_like(rows)
    return jnp.concatenate([jnp.where(head == h, rows, zero) for h in range(4)], 0)


def gather_heads(rows):
    head = lax.broadcasted_iota(jnp.int32, (KEYS, LANES), 1) // HEAD_DIM
    out = rows[:KEYS]
    for h in range(1, 4):
        out = jnp.where(head == h, rows[SLOT * h : SLOT * h + KEYS], out)
    return out


def to_windows(ref, slot, part):
    parted = part.reshape(CELLS, 2, 8, LANES)
    for cg in range(2):
        ref[cg, slot, 0 : CELLS * 8, :] = parted[:, cg].reshape(CELLS * 8, LANES)


def from_windows(ref, slot):
    parts = [ref[cg, slot, 0 : CELLS * 8, :].reshape(CELLS, 1, 8, LANES) for cg in range(2)]
    return jnp.concatenate(parts, 1).reshape(ROWS, LANES)


def cells(shifted):
    win = lax.axis_index("win")
    j = lax.broadcasted_iota(jnp.int32, (KEYS, LANES), 0)
    i = lax.broadcasted_iota(jnp.int32, (KEYS, LANES), 1) % SLOT
    top, left = WINDOW * (win // 2), WINDOW * (win % 2)
    places = [top + j // WINDOW, left + j % WINDOW, top + i // WINDOW, left + i % WINDOW]
    if not shifted:
        return places, None
    region = [(v >= SIDE - WINDOW).astype(jnp.int32) + (v >= SIDE - SHIFT).astype(jnp.int32) for v in places]
    apart = (region[0] != region[2]) | (region[1] != region[3])
    moved = [jnp.where(v + SHIFT >= SIDE, v + SHIFT - SIDE, v + SHIFT) for v in places]
    return moved, jnp.where(apart, NEG, 0.0)


def forward(step, block, shifted, x, refs, keep_n1=None, keep_n2=None, keep_gelu=None, keep_u=None):
    (ext, gain, beta, wqkv, qvb, bias, wp, ob, w1, b1, w2, xs, qw, ss, pr, os, o16, mid) = refs
    xh, _ = norm(x)
    n1 = (xh * gain[block, 0:1, :] + beta[block, 0:1, :]).astype(bf16)
    if keep_n1 is not None:
        keep_n1[step] = n1
    proj = mm(n1, wqkv[...])
    q = (proj[:, :D] + qvb[block, 0:1, :]) * (SCALE * LOG2E)
    k = proj[:, D : 2 * D]
    v = proj[:, 2 * D :] + qvb[block, 1:2, :]
    for g in range(GROUPS):
        cut = slice(LANES * g, LANES * (g + 1))
        to_windows(xs, g, q[:, cut])
        to_windows(xs, GROUPS + g, k[:, cut])
        to_windows(xs, 2 * GROUPS + g, v[:, cut])
    places, apart = cells(shifted)
    if apart is not None:
        apart = jnp.concatenate([apart, apart], 1)

    def scores(w, carry):
        cg, c = w // 8, w % 8
        rows, cols = ext[step * HALF + w, 0], ext[step * HALF + w, 1]
        valid_j = (places[0] < rows) & (places[1] < cols)
        valid_i = (places[2] < rows) & (places[3] < cols)
        mask = jnp.where(valid_i == valid_j, 0.0, NEG)
        mask = jnp.concatenate([mask, mask], 1)
        if apart is not None:
            mask = mask + apart
        for g in range(GROUPS):
            qs, ks, vs = (
                xs[cg, GROUPS * n + g, pl.ds(c, SLOT, stride=8), :].astype(bf16) for n in range(3)
            )
            qw[w, g] = qs
            qw[w, GROUPS + g] = ks
            qw[w, 2 * GROUPS + g] = vs
            ss[w, g] = mm_bt(ks[:KEYS], spread(qs)) + bias[g] + mask
        return carry

    lax.fori_loop(0, HALF, scores, 0, unroll=2)

    def softmax(w, carry):
        for g in range(GROUPS):
            s = ss[w, g]
            e = jnp.exp2(s - jnp.max(s, 0, keepdims=True))
            pr[w, g] = (e * (1.0 / jnp.sum(e, 0, keepdims=True))).astype(bf16)
        return carry

    lax.fori_loop(0, HALF, softmax, 0)

    def mix(w, carry):
        cg, c = w // 8, w % 8
        for g in range(GROUPS):
            os[cg, g, pl.ds(c, KEYS, stride=8), :] = gather_heads(
                mm_at(pr[w, g], qw[w, 2 * GROUPS + g][:KEYS])
            )
        return carry

    lax.fori_loop(0, HALF, mix, 0)
    for g in range(GROUPS):
        o16[:, LANES * g : LANES * (g + 1)] = from_windows(os, g).astype(bf16)
    middle = x + (mm(o16[...], wp[...]) + ob[block, 0:1, :])
    mid[...] = middle
    xh2, _ = norm(middle)
    n2 = (xh2 * gain[block, 1:2, :] + beta[block, 1:2, :]).astype(bf16)
    if keep_n2 is not None:
        keep_n2[step] = n2
    y = middle + ob[block, 1:2, :]
    for part in range(3):
        cut = slice(512 * part, 512 * (part + 1))
        u = mm(n2, w1[:, cut]) + b1[block : block + 1, cut]
        if keep_u is not None:
            keep_u[:, cut] = u.astype(bf16)
        z, phi = gelu(u)
        z = z.astype(bf16)
        if keep_gelu is not None:
            keep_gelu[0][step, :, cut] = z
            keep_gelu[1][:, cut] = gelu_slope(u, phi).astype(bf16)
        y = y + mm(z, w2[cut, :])
    return y


def no_tick(point):
    pass


def mlp_back(step, block, mid, dy, refs, slope, keep_n2=None, beta=None, tick=no_tick):
    (gain, wp, w1, w2, dos, dm_all, du_all, da_all, small) = refs

    def add_small(row, value):
        small[row : row + 1, :] += value

    dm = dy.astype(bf16)
    dm_all[step] = dm
    add_small(7, jnp.sum(dm.astype(f32), 0, keepdims=True))
    dn2 = jnp.zeros((ROWS, D), f32)
    for part in range(4):
        cut = slice(384 * part, 384 * (part + 1))
        du = (mm_bt(dm, w2[cut, :]) * slope(cut)).astype(bf16)
        du_all[step, :, cut] = du
        add_small(8 + part, jnp.sum(du.astype(f32), 0, keepdims=True))
        dn2 = dn2 + mm_bt(du, w1[:, cut])
        tick(part)
    xh, rstd = norm(mid)
    if keep_n2 is not None:
        keep_n2[step] = (xh * gain[block, 1:2, :] + beta[block, 1:2, :]).astype(bf16)
    dx, dgain, dbeta = norm_back(xh, rstd, dn2, gain[block, 1:2, :])
    add_small(1, dgain)
    add_small(3, dbeta)
    dmid = dy + dx
    da = dmid.astype(bf16)
    da_all[step] = da
    add_small(6, jnp.sum(da.astype(f32), 0, keepdims=True))
    do = mm_bt(da, wp[...])
    for g in range(GROUPS):
        to_windows(dos, g, do[:, LANES * g : LANES * (g + 1)])
    tick(4)
    return dmid


def attention_back(step, block, x, dmid, refs, keep_n1=None, beta=None, tick=no_tick):
    (gain, wqkv, xs, qw, pr, dos, dss, dp_all, small, dbias) = refs

    def add_small(row, value):
        small[row : row + 1, :] += value

    def probs_back(w, carry):
        cg, c = w // 8, w % 8
        for g in range(GROUPS):
            d = spread(dos[cg, g, pl.ds(c, SLOT, stride=8), :].astype(bf16))
            p16 = pr[w, g]
            p = p16.astype(f32)
            t = p * mm_bt(qw[w, 2 * GROUPS + g][:KEYS], d)
            ds = (t - p * jnp.sum(t, 0, keepdims=True)).astype(bf16)
            dss[w, g] = ds
            dbias[g] += ds.astype(f32)
            xs[cg, 2 * GROUPS + g, pl.ds(c, KEYS, stride=8), :] = mm(p16, d)
        return carry

    def scores_back(w, carry):
        cg, c = w // 8, w % 8
        for g in range(GROUPS):
            ds = dss[w, g]
            dk = mm(ds, spread(qw[w, g])) * (1.0 / LOG2E)
            dq = gather_heads(mm_at(ds, qw[w, GROUPS + g][:KEYS])) * SCALE
            xs[cg, g, pl.ds(c, KEYS, stride=8), :] = dq
            xs[cg, GROUPS + g, pl.ds(c, KEYS, stride=8), :] = dk
        return carry

    for part in range(2):
        lax.fori_loop(8 * part, 8 * (part + 1), probs_back, 0, unroll=2)
        tick(part)
    for part in range(2):
        lax.fori_loop(8 * part, 8 * (part + 1), scores_back, 0)
        tick(2 + part)
    for n in range(3 * GROUPS):
        dp_all[step, :, LANES * n : LANES * (n + 1)] = from_windows(xs, n).astype(bf16)
    dp = dp_all[step, :, : 3 * D]
    add_small(4, jnp.sum(dp[:, :D].astype(f32), 0, keepdims=True))
    add_small(5, jnp.sum(dp[:, 2 * D :].astype(f32), 0, keepdims=True))
    dn1 = mm_bt(dp, wqkv[...])
    tick(4)
    xh, rstd = norm(x)
    if keep_n1 is not None:
        keep_n1[step] = (xh * gain[block, 0:1, :] + beta[block, 0:1, :]).astype(bf16)
    dx, dgain, dbeta = norm_back(xh, rstd, dn1, gain[block, 0:1, :])
    add_small(0, dgain)
    add_small(2, dbeta)
    tick(5)
    return dmid() + dx


def flat(ref, cut=slice(None)):
    return ref[:, :, cut].reshape(2 * ROWS, -1)


def put_slabs(out, first, value):
    for j in range(value.shape[1] // D):
        out[D * (first + j) : D * (first + j + 1), :] = value[:, D * j : D * (j + 1)].astype(bf16)


def fc_grads(n2, z, dm, du, out, tick=no_tick):
    for first, left, right in ((0, n2, du), (4, dm, z)):
        for j in range(2):
            put_slabs(out, first + 2 * j, mm_at(flat(left), flat(right, slice(768 * j, 768 * (j + 1)))))
        tick(first // 4)


def attention_grads(n1, o16, da, dp, out):
    put_slabs(out, 8, mm_at(flat(n1), flat(dp, slice(3 * D))))
    put_slabs(out, 11, mm_at(flat(o16), flat(da)))


def small_grads(small, dbias, out):
    base = SLABS * D
    out[base : base + SMALL, :] = small[...].astype(bf16)
    out[base + SMALL : SUMS, :] = jnp.zeros((SUMS - base - SMALL, D), bf16)
    out[base + SMALL : base + SMALL + TABLE, : 4 * SLOT] = dbias[...].reshape(TABLE, 4 * SLOT).astype(bf16)


KEEP = WINDOW - SHIFT
NEAR, FAR = slice(0, KEEP), slice(KEEP, WINDOW)
HERE, THERE = slice(SHIFT, WINDOW), slice(0, SHIFT)


def shift_peers():
    win = lax.axis_index("win")
    beside = 1 - 2 * (win % 2)
    below = 2 - 4 * (win // 2 % 2)
    return [{"win": win + beside}, {"win": win + below}, {"win": win + beside + below}]


def shift_copies(source, target, send, recv, back=False):
    plain = [(HERE, HERE), (HERE, THERE), (THERE, HERE), (THERE, THERE)]
    moved = [(NEAR, NEAR), (NEAR, FAR), (FAR, NEAR), (FAR, FAR)]
    if back:
        plain, moved = moved, plain
    out = [pltpu.make_async_copy(source.at[plain[0]], target.at[moved[0]], send.at[3])]
    for n, to in enumerate(shift_peers()):
        out.append(
            pltpu.make_async_remote_copy(
                source.at[plain[n + 1]], target.at[moved[n + 1]], send.at[n], recv.at[n], device_id=to, device_id_type=MESH
            )
        )
    return out


def start_all(copies):
    for copy in copies:
        copy.start()


def wait_all(copies):
    for copy in copies:
        copy.wait()


def greet(peers):
    barrier = pltpu.get_barrier_semaphore()
    for to in peers:
        pl.semaphore_signal(barrier, inc=1, device_id=to, device_id_type=MESH)
    pl.semaphore_wait(barrier, len(peers))


def first_kernel(
    ext, x_ref, cot, gain, beta, wqkv, qvb, bias, wp, ob, w1, b1, w2,
    y_shifted, y_last, cot_shifted, qw, pr, o16, mid, u_ref, xs, ss, os, y_first, send, recv,
):
    step = pl.program_id(0)
    cot_copies = shift_copies(cot, cot_shifted, send.at[0], recv.at[0])
    y_copies = shift_copies(y_first, y_shifted, send.at[1], recv.at[1])

    @pl.when(step == 0)
    def _():
        greet(shift_peers())
        start_all(cot_copies)
        xs[...] = jnp.zeros_like(xs)

    x = x_ref[...].reshape(ROWS, D).astype(f32)
    y = forward(
        step, 0, False, x, (ext, gain, beta, wqkv, qvb, bias, wp, ob, w1, b1, w2, xs, qw, ss, pr, os, o16, mid), keep_u=u_ref
    )
    y = y.astype(bf16).reshape(WINDOW, WINDOW, HALF, D)

    @pl.when(step == 0)
    def _():
        y_first[...] = y
        start_all(y_copies)

    @pl.when(step == 1)
    def _():
        y_last[...] = y
        wait_all(y_copies)
        wait_all(cot_copies)


def second_kernel(
    ext, count, x_first, x_last, cot_ref, gain, beta, wqkv, qvb, bias, wp, ob, w1, b1, w2,
    y_ref, dx_shifted, dx_last, grads,
    xs, qw, ss, pr, os, mid, slope, dos, dss, small, dbias, n1, n2, o16, z, dm, du, da, dp, x_both, dx_first, send, recv, local,
):
    step = pl.program_id(0)
    x_copies = shift_copies(x_last, x_both.at[1], send.at[0], recv.at[0])
    dx_copies = shift_copies(dx_first, dx_shifted, send.at[1], recv.at[1], back=True)

    @pl.when(step == 0)
    def _():
        load = pltpu.make_async_copy(x_first, x_both.at[0], local)
        load.start()
        greet(shift_peers())
        start_all(x_copies)
        load.wait()
        xs[...] = jnp.zeros_like(xs)
        dos[...] = jnp.zeros_like(dos)
        small[...] = jnp.zeros_like(small)
        dbias[...] = jnp.zeros_like(dbias)

    @pl.when(step == 1)
    def _():
        wait_all(x_copies)

    x = x_both[step].reshape(ROWS, D).astype(f32)
    live = lax.broadcasted_iota(jnp.int32, (CELLS, HALF, 1), 1) + step * HALF < count[0]
    y = forward(
        step, 1, True, x,
        (ext, gain, beta, wqkv, qvb, bias, wp, ob, w1, b1, w2, xs, qw, ss, pr, os, o16.at[step], mid),
        n1, n2, (z, slope),
    )
    y_ref[...] = jnp.where(live, y.reshape(CELLS, HALF, D), 0.0).astype(bf16)
    dy = jnp.where(live, cot_ref[...].astype(f32), 0.0).reshape(ROWS, D)
    mid[...] = mlp_back(
        step, 1, mid[...], dy, (gain, wp, w1, w2, dos, dm, du, da, small), lambda cut: slope[:, cut].astype(f32)
    )
    dx = attention_back(
        step, 1, x, lambda: mid[...], (gain, wqkv, xs, qw, pr, dos, dss, dp, small, dbias)
    )
    dx = dx.astype(bf16).reshape(WINDOW, WINDOW, HALF, D)

    @pl.when(step == 0)
    def _():
        dx_first[...] = dx
        start_all(dx_copies)

    @pl.when(step == 1)
    def _():
        dx_last[...] = dx
        fc_grads(n2, z, dm, du, grads)
        attention_grads(n1, o16, da, dp, grads)
        small_grads(small, dbias, grads)
        wait_all(dx_copies)


def third_kernel(
    x_ref, dy_first, dy_last, y_ref, qw, pr, o_ref, mid, u_ref, gain, beta, wqkv, wp, w1, w2, two_ref,
    dx_ref, one_out, two_out, y_out,
    xs, dos, dss, small, dbias, dmid, n2, o16, z, dm, du, da,
    one, two, land_one, send_one, recv_one, free_one, land_two, send_two, recv_two, free_two, local, loads, dy_both, send, recv,
):
    step = pl.program_id(0)
    first = Exchange(one, land_one, send_one, recv_one, free_one)
    second = Exchange(two, land_two, send_two, recv_two, free_two)
    dy_copies = shift_copies(dy_last, dy_both.at[1], send.at[0], recv.at[0], back=True)
    y_copies = shift_copies(y_ref, y_out, send.at[1], recv.at[1], back=True)
    last = 24
    moves = [[] for _ in range(last + 1)]
    late = []
    for exchange, group, begin, every in ((second, 0, 0, 3), (second, 1, 1, 3), (second, 2, 2, 3), (first, 0, 12, 2), (first, 1, 13, 2)):
        for k in range(exchange.stages + 1):
            n = begin + every * k
            (moves[n] if n <= last else late).append((exchange, group, k))

    def tick(n):
        for exchange, group, k in moves[n]:
            exchange.advance(GROUPED[group], k)

    def tick_at(steps, base, per_step):
        def ticker(point):
            for s in steps:
                pl.when(step == s)(lambda s=s: tick(base + (s - steps[0]) * per_step + point))

        return ticker

    def kept(half):
        rows = pl.ds(half * ROWS, ROWS)
        return (
            pltpu.make_async_copy(u_ref.at[rows], z.at[half], loads.at[0, half]),
            pltpu.make_async_copy(o_ref.at[rows], o16.at[half], loads.at[1, half]),
        )

    @pl.when(step == 0)
    def _():
        load = pltpu.make_async_copy(two_ref, two, local.at[0])
        load.start()
        load_dy = pltpu.make_async_copy(dy_first, dy_both.at[0], local.at[1])
        load_dy.start()
        for half in range(2):
            start_all(kept(half))
        greet(second.peers() + shift_peers()[2:])
        start_all(dy_copies)
        xs[...] = jnp.zeros_like(xs)
        dos[...] = jnp.zeros_like(dos)
        small[...] = jnp.zeros_like(small)
        dbias[...] = jnp.zeros_like(dbias)
        load.wait()
        tick(0)
        start_all(y_copies)
        load_dy.wait()

    for half in range(2):

        @pl.when(step == half)
        def _():
            wait_all(kept(half))
            if half:
                wait_all(dy_copies)

    @pl.when(step < 2)
    def _():
        def slope(cut):
            u = z[step, :, cut].astype(f32)
            value, phi = gelu(u)
            z[step, :, cut] = value.astype(bf16)
            return gelu_slope(u, phi)

        dmid[step] = mlp_back(
            step, 0, mid[...], dy_both[step].astype(f32).reshape(ROWS, D),
            (gain, wp, w1, w2, dos.at[step], dm, du, da, small), slope, n2, beta, tick_at((0, 1), 1, 5),
        )

    @pl.when(step == 1)
    def _():
        fc_grads(n2, z, dm, du, one, lambda point: tick(11 + point))

    @pl.when(step >= 2)
    def _():
        half = step - 2
        dx = attention_back(
            half, 0, x_ref[...].reshape(ROWS, D).astype(f32), lambda: dmid[half],
            (gain, wqkv, xs, qw, pr, dos.at[half], dss, du, small, dbias), n2, beta, tick_at((2, 3), 13, 6),
        )
        dx_ref[...] = dx.astype(bf16).reshape(dx_ref.shape)

    @pl.when(step == 3)
    def _():
        for exchange, group, k in late:
            if exchange is second:
                exchange.advance(GROUPED[group], k)
        store_two = pltpu.make_async_copy(two, two_out, local.at[0])
        store_two.start()
        attention_grads(n2, o16, da, du, one)
        small_grads(small, dbias, one)
        first.advance(GROUPED[2], 0)
        for exchange, group, k in late:
            if exchange is first:
                exchange.advance(GROUPED[group], k)
        for k in range(1, first.stages + 1):
            first.advance(GROUPED[2], k)
        store_one = pltpu.make_async_copy(one, one_out, local.at[1])
        store_one.start()
        wait_all(y_copies)
        store_one.wait()
        store_two.wait()


def whole(shape):
    return pl.BlockSpec(shape, lambda s: (0,) * len(shape), pipeline_mode=pl.Buffered(1))


def of_block(block, *shape):
    return pl.BlockSpec((None,) + shape, lambda s: (block,) + (0,) * len(shape), pipeline_mode=pl.Buffered(1))


def by_half(*shape, buffers=2):
    return pl.BlockSpec(shape, lambda s: (s,) + (0,) * (len(shape) - 1), pipeline_mode=pl.Buffered(buffers))


ANY_SPEC = pl.BlockSpec(memory_space=pl.ANY)
SMEM_SPEC = pl.BlockSpec(memory_space=pltpu.SMEM)
TOKEN_SPEC = pl.BlockSpec((CELLS, HALF, D), lambda s: (0, s, 0))
XS = VMEM((2, 3 * GROUPS, 8 * SLOT, LANES), f32)
DOS = VMEM((2, GROUPS, 8 * SLOT, LANES), f32)
QW = (HALF, 3 * GROUPS, SLOT, LANES)
PR = (HALF, GROUPS, KEYS, 4 * SLOT)


def params(collective_id=None, mib=61):
    return pltpu.CompilerParams(
        vmem_limit_bytes=mib * 2**20, dimension_semantics=("arbitrary",), collective_id=collective_id,
        has_side_effects=collective_id is not None,
    )


CELL = (WINDOW, WINDOW)
PART = jax.ShapeDtypeStruct(CELL + (HALF, D), bf16)
SHIFTS = [pltpu.SemaphoreType.DMA((2, 4)), pltpu.SemaphoreType.DMA((2, 4))]


def run_first(ext, x, cot, gain, beta, wqkv, qvb, bias, wp, ob, w1, b1, w2):
    crops = x.shape[1]
    return pl.pallas_call(
        first_kernel,
        grid=(2,),
        out_shape=(
            PART,
            PART,
            jax.ShapeDtypeStruct(cot.shape, bf16),
            jax.ShapeDtypeStruct((crops,) + QW[1:], bf16),
            jax.ShapeDtypeStruct((crops,) + PR[1:], bf16),
            jax.ShapeDtypeStruct((2 * ROWS, D), bf16),
            jax.ShapeDtypeStruct((2 * ROWS, D), f32),
            jax.ShapeDtypeStruct((2 * ROWS, FF), bf16),
        ),
        in_specs=[
            SMEM_SPEC, TOKEN_SPEC, ANY_SPEC, whole(gain.shape), whole(beta.shape), of_block(0, D, 3 * D), whole(qvb.shape),
            of_block(0, GROUPS, KEYS, 4 * SLOT), of_block(0, D, D), whole(ob.shape), of_block(0, D, FF),
            whole(b1.shape), of_block(0, FF, D),
        ],
        out_specs=(
            ANY_SPEC, whole(PART.shape), ANY_SPEC, by_half(*QW), by_half(*PR), by_half(ROWS, D), by_half(ROWS, D),
            by_half(ROWS, FF),
        ),
        scratch_shapes=[
            XS, VMEM(PR, f32), VMEM((2, GROUPS, 8 * KEYS, LANES), f32), VMEM(PART.shape, bf16),
        ] + SHIFTS,
        compiler_params=params(1),
        name="first_forward",
    )(ext, x, cot, gain, beta, wqkv, qvb, bias, wp, ob, w1, b1, w2)


GRADS = jax.ShapeDtypeStruct((SUMS, D), bf16)
SMALLS = [VMEM((SMALL, D), f32), VMEM((GROUPS, KEYS, 4 * SLOT), f32)]


def run_second(ext, count, x_first, x_last, cot, gain, beta, wqkv, qvb, bias, wp, ob, w1, b1, w2):
    return pl.pallas_call(
        second_kernel,
        grid=(2,),
        out_shape=(jax.ShapeDtypeStruct(cot.shape, bf16), PART, PART, GRADS),
        in_specs=[
            SMEM_SPEC, SMEM_SPEC, ANY_SPEC, ANY_SPEC, TOKEN_SPEC, whole(gain.shape), whole(beta.shape), of_block(1, D, 3 * D),
            whole(qvb.shape), of_block(1, GROUPS, KEYS, 4 * SLOT), of_block(1, D, D), whole(ob.shape),
            of_block(1, D, FF), whole(b1.shape), of_block(1, FF, D),
        ],
        out_specs=(TOKEN_SPEC, ANY_SPEC, whole(PART.shape), whole(GRADS.shape)),
        scratch_shapes=[
            XS, VMEM(QW, bf16), VMEM(PR, f32), VMEM(PR, bf16), VMEM((2, GROUPS, 8 * KEYS, LANES), f32),
            VMEM((ROWS, D), f32), VMEM((ROWS, FF), bf16), DOS, VMEM(PR, bf16),
        ] + SMALLS + [VMEM((2, ROWS, width), bf16) for width in (D, D, D, FF, D, FF, D, 3 * D)]
        + [VMEM((2,) + PART.shape, bf16), VMEM(PART.shape, bf16)] + SHIFTS + [pltpu.SemaphoreType.DMA(())],
        compiler_params=params(2, 63),
        name="second_block",
    )(ext, count, x_first, x_last, cot, gain, beta, wqkv, qvb, bias, wp, ob, w1, b1, w2)


def in_steps(first, *shape, axis=0, buffers=2):
    def index(s):
        return tuple(jnp.clip(s - first, 0, 1) if n == axis else 0 for n in range(len(shape)))

    return pl.BlockSpec(shape, index, pipeline_mode=pl.Buffered(buffers))


def run_third(x, dy_first, dy_last, y, qw, pr, o16, mid, u, gain, beta, wqkv, wp, w1, w2, two):
    tokens = (CELLS, HALF, D)
    return pl.pallas_call(
        third_kernel,
        grid=(4,),
        out_shape=(jax.ShapeDtypeStruct(x.shape, bf16), GRADS, GRADS, jax.ShapeDtypeStruct(y.shape, bf16)),
        in_specs=[
            in_steps(2, *tokens, axis=1), ANY_SPEC, ANY_SPEC, ANY_SPEC, in_steps(2, *QW, buffers=1),
            in_steps(2, *PR, buffers=1), ANY_SPEC, in_steps(0, ROWS, D), ANY_SPEC,
            whole(gain.shape), whole(beta.shape), of_block(0, D, 3 * D), of_block(0, D, D), of_block(0, D, FF),
            of_block(0, FF, D), ANY_SPEC,
        ],
        out_specs=(in_steps(2, *tokens, axis=1), ANY_SPEC, ANY_SPEC, ANY_SPEC),
        scratch_shapes=[XS, VMEM((2,) + DOS.shape, f32), VMEM(PR, bf16)] + SMALLS + [VMEM((2, ROWS, D), f32)]
        + [VMEM((2, ROWS, width), bf16) for width in (D, D, FF, D, FF, D)]
        + [VMEM(GRADS.shape, bf16)] * 2 + exchange_scratch() * 2
        + [pltpu.SemaphoreType.DMA((2,)), pltpu.SemaphoreType.DMA((2, 2)), VMEM((2,) + PART.shape, bf16)] + SHIFTS,
        compiler_params=params(0, 63),
        name="first_backward",
    )(x, dy_first, dy_last, y, qw, pr, o16, mid, u, gain, beta, wqkv, wp, w1, w2, two)


def jobs():
    n_img, n_win = lax.axis_size("img"), lax.axis_size("win")
    bits = [("win", b) for b in range(1, n_win.bit_length() - 1)] + [("img", b) for b in range(n_img.bit_length() - 1)]
    pairs = [bits[n : n + 2] for n in range(0, len(bits), 2)]
    orders = [[[("win", 0)]] + pairs, [[("win", 0)]] + pairs[::-1]]
    out = []
    for group in range(3):
        out += [(1536 * group, 1024, orders[0]), (1536 * group + 1024, 512, orders[1])]
    return out + [(SLABS * D, SUMS - SLABS * D, orders[0])]


def plan_sizes(size, order):
    out = []
    for group in order:
        ways = 2 ** len(group)
        cut = ways if size % (16 * ways) == 0 else 1
        size //= cut
        out.append((ways, cut, size))
    return out


class Exchange:
    def __init__(self, buf, landing, send, recv, free):
        self.buf, self.landing, self.send, self.recv, self.free = buf, landing, send, recv, free
        index = {axis: lax.axis_index(axis) for axis in ("img", "win")}
        self.plans, land = [], 0
        for start, rows, order in jobs():
            plan = []
            for group, (ways, cut, size) in zip(order, plan_sizes(rows, order)):
                own = [(index[axis] // 2**bit) % 2 for axis, bit in group]
                peers = []
                for apart in range(1, ways):
                    to, piece = {}, 0
                    for n, (axis, bit) in enumerate(group):
                        here = own[n]
                        if apart >> n & 1:
                            to[axis] = to.get(axis, index[axis]) + 2**bit - 2 ** (bit + 1) * here
                            here = 1 - here
                        piece = piece + here * 2**n
                    peers.append((to, start + piece * size if cut > 1 else start, land))
                    land += size
                if cut > 1:
                    start = start + sum(here * 2**n for n, here in enumerate(own)) * size
                plan.append((start, size, cut, peers))
            self.plans.append(plan)
        self.bits = len(self.plans[0])
        self.stages = 2 * self.bits

    def peers(self):
        return [to for *_, peers in self.plans[0] for to, _, _ in peers]

    def copies(self, c, k):
        n = min(k, self.stages - 1 - k)
        keep, size, cut, peers = self.plans[c][n]
        if k >= self.bits and cut == 1:
            return []
        out = []
        for p, (to, give, land) in enumerate(peers):
            if k < self.bits:
                source, target = self.buf.at[pl.ds(pl.multiple_of(give, 16), size)], self.landing.at[pl.ds(land, size)]
            else:
                source = target = self.buf.at[pl.ds(pl.multiple_of(keep, 16), size)]
            out.append(
                pltpu.make_async_remote_copy(
                    source, target, self.send.at[c, k, p], self.recv.at[c, k, p], device_id=to, device_id_type=MESH
                )
            )
        return out

    def start(self, c, k):
        copies = self.copies(c, k)
        if copies and k >= self.bits:
            pl.semaphore_wait(self.free.at[c, self.stages - 1 - k], len(copies))
        for copy in copies:
            copy.start()

    def finish(self, c, k):
        for copy in self.copies(c, k):
            copy.wait()
        if k >= self.bits:
            return
        keep, size, cut, peers = self.plans[c][k]
        if cut > 1:
            for to, _, _ in peers:
                pl.semaphore_signal(self.free.at[c, k], inc=1, device_id=to, device_id_type=MESH)
        tile = max(t for t in (16, 32, 48, 64) if size % t == 0)

        def add(i, carry):
            here = pl.ds(pl.multiple_of(keep + i * tile, 16), tile)
            total = self.buf[here, :].astype(f32)
            for _, _, land in peers:
                total = total + self.landing[pl.ds(pl.multiple_of(land + i * tile, 16), tile), :].astype(f32)
            self.buf[here, :] = total.astype(bf16)
            return carry

        lax.fori_loop(0, size // tile, add, 0)

    def advance(self, which, k):
        for c in which:
            if 1 <= k <= self.stages:
                self.finish(c, k - 1)
            if k < self.stages:
                self.start(c, k)


def exchange_scratch():
    landing, most = 0, 0
    for _, rows, order in jobs():
        for ways, _, size in plan_sizes(rows, order):
            landing += size * (ways - 1)
            most = max(most, ways - 1)
    n, bits = len(jobs()), len(jobs()[0][2])
    dma = pltpu.SemaphoreType.DMA((n, 2 * bits, most))
    return [VMEM((landing, D), bf16), dma, dma, pltpu.SemaphoreType.REGULAR((n, bits))]


def finish_kernel(*refs):
    ins, outs = refs[:8], refs[8:]
    for n, out in enumerate(outs):
        for block in range(2):
            value = ins[2 * n + block][...].astype(f32)
            out[block] = value.T if n == 1 else value


def finish(grads_one, grads_two):
    slabs = [lambda j: (j, 0), lambda j: (4 + j, 0), lambda j: (8 + jnp.minimum(j, 2), 0), lambda j: (11, 0)]
    targets = [lambda j: (0, 0, j), lambda j: (0, j, 0), lambda j: (0, 0, jnp.minimum(j, 2)), lambda j: (0, 0, 0)]
    return pl.pallas_call(
        finish_kernel,
        grid=(4,),
        out_shape=tuple(jax.ShapeDtypeStruct((2,) + s, f32) for s in ((D, FF), (FF, D), (D, 3 * D), (D, D))),
        in_specs=[pl.BlockSpec((D, D), index) for index in slabs for _ in range(2)],
        out_specs=tuple(pl.BlockSpec((2, D, D), index) for index in targets),
        compiler_params=params(),
        name="finish_gradients",
    )(*[grads_one, grads_two] * 4)


def position_lookup():
    j = jnp.arange(KEYS)[:, None]
    i = jnp.arange(SLOT)[None, :]
    side = SIDE - 1
    index = (i // WINDOW - j // WINDOW + WINDOW - 1) * side + i % WINDOW - j % WINDOW + WINDOW - 1
    index = jnp.where((i < CELLS) & (j < CELLS), index, -1).reshape(-1)
    return (jnp.arange(side * side)[:, None] == index[None, :]).astype(f32)


def on_device(
    tokens, cotangent, crop_counts, crop_extent, norm_gain, norm_bias, qkv_weight, qv_bias, rel_table, proj_weight,
    out_bias, fc1_weight, fc1_bias, fc2_weight,
):
    crops = tokens.shape[0]
    x = tokens.reshape(crops, CELLS, D).transpose(1, 0, 2)
    cot = cotangent.reshape(crops, CELLS, D).transpose(1, 0, 2)
    lookup = position_lookup()
    highest = lax.Precision.HIGHEST
    bias = jnp.einsum("bkh,kp->bhp", rel_table, lookup, precision=highest) * LOG2E
    bias = bias.reshape(2, GROUPS, 4, KEYS, SLOT).transpose(0, 1, 3, 2, 4)
    bias = jnp.where(jnp.arange(KEYS)[:, None, None] < CELLS, bias, NEG).reshape(2, GROUPS, KEYS, 4 * SLOT)

    cells_of = lambda v: v.reshape(CELL + v.shape[1:])
    rows_of = lambda v: v.reshape((CELLS,) + v.shape[2:])
    x_first, x_last, cot_shifted, qw, pr, o16, mid, u = run_first(
        crop_extent, x, cells_of(cot), norm_gain, norm_bias, qkv_weight, qv_bias, bias, proj_weight, out_bias,
        fc1_weight, fc1_bias, fc2_weight,
    )
    y, dx_first, dx_last, grads_two = run_second(
        crop_extent, crop_counts, x_first, x_last, rows_of(cot_shifted), norm_gain, norm_bias, qkv_weight, qv_bias,
        bias, proj_weight, out_bias, fc1_weight, fc1_bias, fc2_weight,
    )
    dx, sum_one, sum_two, output = run_third(
        x, dx_first, dx_last, cells_of(y), qw, pr, o16, mid, u, norm_gain, norm_bias, qkv_weight, proj_weight,
        fc1_weight, fc2_weight, grads_two,
    )
    fc1, fc2, qkv, proj = finish(sum_one, sum_two)
    rows = jnp.stack([sum_one[SLABS * D :], sum_two[SLABS * D :]]).astype(f32)
    dbias = rows[:, SMALL : SMALL + TABLE, : 4 * SLOT].reshape(2, GROUPS, KEYS, 4, SLOT).transpose(0, 1, 3, 2, 4)
    table = jnp.einsum("hp,kp->kh", dbias.reshape(2 * HEADS, KEYS * SLOT), lookup, precision=highest)
    table = table.reshape(-1, 2, HEADS).transpose(1, 0, 2)
    back = lambda v: v.transpose(1, 0, 2).reshape(tokens.shape)
    return (
        back(rows_of(output)), back(dx), rows[:, 0:2], rows[:, 2:4], qkv, rows[:, 4:6], table, proj, rows[:, 6:8], fc1,
        rows[:, 8:12].reshape(2, FF), fc2,
    )


def solution(mesh):
    split = P("img", "win", None, None)
    return jax.shard_map(
        on_device,
        mesh=mesh,
        in_specs=(split, split, P("img"), P("img", None)) + (P(),) * 10,
        out_specs=(split, split) + (P(),) * 10,
        check_vma=False,
    )
```

time: 343 us -> 278 us (0.81)
  waiting for transfers between devices: 32.5 us -> 0 us
  other arithmetic: 11.9 us -> 0.33 us
  local copies, waits for them, and re-layouts: 18 us -> 10.5 us
  starting transfers between devices: 6.78 us -> 0 us
  Pallas kernels: 267 us -> 263 us
    ppermute x8 -> x0, waiting for transfers between devices: 32.5 us -> none  [partner(): return lax.ppermute(value, 'win', pairs)]
    concatenate x9 -> x0, other arithmetic: 7.93 us -> none  [the longest x2 4.52 us: shift_out(): jnp.concatenate([partner(widened[keep:], 1), widened[:keep]], 0)]
    ppermute x8 -> x0, starting transfers between devices: 6.78 us -> none  [partner(): return lax.ppermute(value, 'win', pairs)]
    pallas_call x3 -> x2, Pallas kernels: 181 us -> 176 us  [the longest x1 141 us: run_third(): pl.pallas_call(third_kernel, grid=(4,), out_shape=(jax.ShapeDtypeStruct(x...]
    slice x10 -> x0, local copies, waits for them, and re-layouts: 3.95 us -> none  [the longest x4 2.53 us: shift_out(): widened = jnp.concatenate([partner(grid[:, keep:], 0), grid[:, :keep]], 1)]
  transfers between devices with their start and end apart: 8 -> 0, of which waited for: 4 -> 0; matrix products, arithmetic and copies ran while one was open for 6% -> 0% of each run, Pallas kernels for 46% -> 0%
where the time goes in v2:
time: 278 us
  Pallas kernels  263 us (95%)
  local copies, waits for them, and re-layouts  10.5 us (4%)
    pallas_call x1, Pallas kernels, run_third(): pl.pallas_call(third_kernel, grid=(4,), out_shape=(jax.ShapeDtypeStruct(x...  141 us
    pallas_call x1, Pallas kernels, run_second(): pl.pallas_call(second_kernel, grid=(2,), out_shape=(jax.ShapeDtypeStruct(...  78.6 us
    pallas_call x1, Pallas kernels, run_first(): pl.pallas_call(first_kernel, grid=(2,), out_shape=(PART, PART, jax.ShapeD...  35.5 us
    pallas_call x1, Pallas kernels, finish(): pl.pallas_call(finish_kernel, grid=(4,), out_shape=tuple((jax.ShapeDtypeS...  8.73 us

profile of v2, /device:TPU:0, one launch (start us, length us, event | category | flops | bytes accessed | tf_op | source)
XLA Modules:
  0.0 277.6 jit_solution(41877741405299727)
XLA Ops:
  1.4 1.4 copy.36.ext
  2.7 0.1 add_select_fusion
  2.8 0.1 reshape.215
  2.9 1.1 fusion
  4.0 0.3 copy.33
  4.3 0.4 reshape.202
  4.7 0.1 select_bitcast_fusion
  4.9 0.3 copy.34
  5.1 1.2 reshape.203.bias
  6.3 35.5 %first_forward.1 = (bf16[7,7,16,384]{3,2,1,0:T(8,128)(2,1)}, bf16[7,7,16,384]{3,2,1,0:T(8,128)(2,1)}, bf16[7,7,32,384]{3,2,1,0:T(8,128)(2,1)}, bf16[32,9,64,128]...) custom-call(s32[32,2]{1,0:T(8,128)} %copy.36.ext, ...), custom_call_target="tpu_custom_call" | custom-call | tf_op jit(solution)/shard_map/first_forward/pallas_call | solution.py:589
  41.8 78.6 %second_block.1 = (bf16[49,32,384]{2,1,0:T(8,128)(2,1)}, bf16[7,7,16,384]{3,2,1,0:T(8,128)(2,1)}, bf16[7,7,16,384]{3,2,1,0:T(8,128)(2,1)}, bf16[4864,384]{1,0:T(8,128)(2,1)}) custom-call(s32[32,2]{1,0:T(8,128)} %copy.36.ext, s32[1]{0:T(128)S(6)} %copy.49.count, bf16[7,7,16,384]{3,2,1,0:T(8,128)(2,1)} %get-tuple-element.32.x_first, ...), custom_call_target="tpu_custom_call" | custom-call | tf_op jit(solution)/shard_map/second_block/pallas_call | solution.py:624
  120.4 140.6 %first_backward.1 = (bf16[49,32,384]{2,1,0:T(8,128)(2,1)}, bf16[4864,384]{1,0:T(8,128)(2,1)}, bf16[4864,384]{1,0:T(8,128)(2,1)}, bf16[7,7,32,384]{3,2,1,0:T(8,128)(2,1)}) custom-call(bf16[49,32,384]{2,1,0:T(8,128)(2,1)} %bitcast.47, bf16[7,7,16,384]{3,2,1,0:T(8,128)(2,1)} %get-tuple-element.35.dy_first, bf16[7,7,16,384]{3,2,1,0:T(8,128)(2,1)} %get-tuple-element.36.dy_last, ...), custom_call_target="tpu_custom_call" | custom-call | tf_op jit(solution)/shard_map/first_backward/pallas_call | solution.py:653
  261.0 0.9 slice_bitcast_fusion.1
  261.9 0.9 slice_bitcast_fusion
  262.9 0.2 reshape.209
  263.2 0.2 dot_general.9
  263.4 0.6 fusion.7
  263.9 0.6 copy.39
  264.7 0.6 fusion.14
  265.3 0.6 copy.40
  265.9 8.7 %finish_gradients.1 = (f32[2,384,1536]{2,1,0:T(8,128)}, f32[2,1536,384]{2,1,0:T(8,128)}, f32[2,384,1152]{2,1,0:T(8,128)}, f32[2,384,384]{2,1,0:T(8,128)}) custom-call(bf16[4864,384]{1,0:T(8,128)(2,1)} %get-tuple-element.46.refs_0_.refs_2_.refs_4_.refs_6_, bf16[4864,384]{1,0:T(8,128)(2,1)} %get-tuple-element.47.refs_1_.refs_3_.refs_5_.refs_7_, ...), custom_call_target="tpu_custom_call" | custom-call | tf_op jit(solution)/shard_map/finish_gradients/pallas_call | solution.py:800
  274.6 1.0 copy.50
  275.7 0.7 copy-done.1
  276.3 1.0 copy.51
  (13 shorter events, 0.2 us)
Async XLA Ops:
  0.6 2.3 copy-start
  265.9 8.7 %copy-start.2 = (bf16[7,7,32,384]{3,2,1,0:T(8,128)(2,1)S(1)}, bf16[7,7,32,384]{3,2,1,0:T(8,128)(2,1)}, u32[]{:S(2)}) copy-start(bf16[7,7,32,384]{3,2,1,0:T(8,128)(2,1)} %get-tuple-element.44) | copy-start | bytes 3612676
  274.6 1.7 copy-start.1
